TPU v7x, 32 devices: a whole 2x2x4 slice. The times are simulated.
32 devices in a mesh: pipe: 2 (over core), dp: 16 (over z, y, x).
Axes of the slice: x: 2, y: 2, z: 4, core: 2. Of those that a mesh axis runs over, the one named last changes fastest.
Arguments:
- images: bfloat16 [128, 16, 16, 1024], P('dp'), may hold values from -25 to 25
- extents: int32 [128, 2], P('dp'), may hold values from 8 to 16, as said below
- views: int32 [128], P('dp'), may hold values from 0 to 1, as said below
- params: bfloat16 [2, 6029312], P('pipe'), may hold values from -0.1875 to 0.1875
- norms: float32 [2, 2, 5120], P('pipe'), may hold values from -2 to 2, as said below
- cotangent: bfloat16 [128, 8, 8, 2048], P('dp'), may hold values from -6 to 6
Outputs:
- boundary: bfloat16 [2, 128, 262144], P('pipe', 'dp')
- weight_grads: float32 [2, 6029312], P('pipe')
- norm_grads: float32 [2, 2, 5120], P('pipe')
Inputs may be any that keep to these rules, and one draw needn't show every extreme that they name: `extents`: entry [i, 0] is image i's valid height and [i, 1] its valid width, even numbers from 8 to 16 and from 8 to 16; the valid region is the top-left corner. The first of every dp index's images is whole. Images 2 k and 2 k + 1 have different views. `norms`: gains lie in 0.5 to 1.5.
All inputs are finite; a program needn't handle non-finite values.
Results may differ from a plain program's by a relative error of at most 0.014.
Values may be sent and summed in bfloat16 or wider, within the bound.
No kernel may reach another device: no remote copies, remote signals or barrier semaphores. Data moves between devices by JAX's collectives and lax.ppermute only.
A program may use at most 384 MiB of HBM per device.

v0:
```python
import jax
import jax.numpy as jnp
from jax import lax
from jax.sharding import PartitionSpec as P

C0 = 1024
M0 = 256
M1 = 512
C1 = 2048
HB = 16
WB = 16
IMG_MB = 2
MB = 4
P_SIZE = 6029312
CN = 5120


EPSILON = 1e-05
PRECISE = lax.Precision.HIGHEST


def from_behind(value, axis, steps):
    count = lax.axis_size(axis)
    pairs = [(source, (source + steps) % count) for source in range(count)]
    return lax.ppermute(value, axis, pairs)


def for_sending(array):

    def short(part):
        return part.astype(jnp.bfloat16) if part.dtype == jnp.float32 else part

    return jax.tree.map(short, array)


def silu_value(values):
    return values * jax.nn.sigmoid(values)


def silu_slope(values):
    sigmoid_v = jax.nn.sigmoid(values)
    return sigmoid_v * (1.0 + values * (1.0 - sigmoid_v))


def section_shape(section_id):
    if section_id == 0:
        return (M0, C0, HB, WB)
    return (M1, C1, HB // 2, WB // 2)


def unpack_weights(packed, section_id):
    middle, outward, height, breadth = section_shape(section_id)
    shapes = [(C0, middle), (9 * middle, middle), (middle, outward)]
    if section_id == 1:
        shapes.append((C0, C1))
    pieces = []
    offset = 0
    for first_dim, second_dim in shapes:
        pieces.append(
            packed[offset : offset + first_dim * second_dim].reshape(first_dim, second_dim)
        )
        offset = offset + first_dim * second_dim
    return pieces


def norm_slices(norm_row, section_id):
    middle, outward, height, breadth = section_shape(section_id)
    bounds = [0, middle, 2 * middle, 2 * middle + outward, 2 * middle + outward + C1]
    count_bn = 3 if section_id == 0 else 4
    return [
        (norm_row[0, bounds[k] : bounds[k + 1]], norm_row[1, bounds[k] : bounds[k + 1]])
        for k in range(count_bn)
    ]


def layout(extents, views, height, breadth):
    row_ids = jnp.arange(height, dtype=jnp.int32)
    col_ids = jnp.arange(breadth, dtype=jnp.int32)
    inside = (row_ids[None, :, None] < extents[:, 0, None, None]) & (
        col_ids[None, None, :] < extents[:, 1, None, None]
    )
    pixel_mask = inside.astype(jnp.float32)
    onehot = (views[:, None] == jnp.arange(2, dtype=jnp.int32)[None, :]).astype(jnp.float32)
    weighted = (pixel_mask[:, :, :, None] * onehot[:, None, None, :]).reshape(-1, 2)
    selector = jnp.broadcast_to(onehot[:, None, None, :], pixel_mask.shape + (2,)).reshape(-1, 2)
    return (pixel_mask.reshape(-1, 1), weighted, selector)


def moments(values, weighted):
    return jnp.stack(
        [
            jnp.dot(weighted.T, values, precision=PRECISE),
            jnp.dot(weighted.T, values * values, precision=PRECISE),
        ]
    )


def back_moments(grad_pre, normed, weighted):
    return jnp.stack(
        [
            jnp.dot(weighted.T, grad_pre, precision=PRECISE),
            jnp.dot(weighted.T, grad_pre * normed, precision=PRECISE),
        ]
    )


def normalize(values, totals, counts, selector):
    average = totals[0] / counts[:, None]
    spread = totals[1] / counts[:, None] - average * average
    inverse_dev = lax.rsqrt(spread + EPSILON)
    scale_pix = jnp.dot(selector, inverse_dev, precision=PRECISE)
    return ((values - jnp.dot(selector, average, precision=PRECISE)) * scale_pix, scale_pix)


def norm_back(grad_out, normed, scale_pix, gain, back_totals, counts, selector, pixel_mask):
    first_avg = jnp.dot(selector, back_totals[0] / counts[:, None], precision=PRECISE)
    second_avg = jnp.dot(selector, back_totals[1] / counts[:, None], precision=PRECISE)
    return pixel_mask * scale_pix * gain * (grad_out - first_avg - normed * second_avg)


def patches(act):
    image_count, height, breadth, channels = act.shape
    padded = jnp.pad(act, ((0, 0), (1, 1), (1, 1), (0, 0)))
    pieces = [padded[:, a : a + height, b : b + breadth, :] for a in range(3) for b in range(3)]
    return jnp.concatenate(pieces, axis=3).reshape(image_count * height * breadth, 9 * channels)


def unpatch(grad_cols, image_count, height, breadth, channels):
    tap_grads = grad_cols.reshape(image_count, height, breadth, 9, channels)
    padded = jnp.zeros((image_count, height + 2, breadth + 2, channels), jnp.float32)
    for a in range(3):
        for b in range(3):
            padded = padded.at[:, a : a + height, b : b + breadth, :].add(
                tap_grads[:, :, :, 3 * a + b, :]
            )
    return padded[:, 1:-1, 1:-1, :].reshape(image_count * height * breadth, channels)


def widen_to(values, width):
    return jnp.pad(values, ((0, 0), (0, 0), (0, width - values.shape[2])))


def micro_slice(array, index):
    return array[index * IMG_MB : (index + 1) * IMG_MB]


def blank_of(values):
    return jax.tree.map(jnp.zeros_like, values)


def by_section(section_index, first, second, first_on, second_on):

    def first_branch():
        made = first()
        if not first_on:
            made = blank_of(made)
        return (made, blank_of(second()))

    def second_branch():
        made = second()
        if not second_on:
            made = blank_of(made)
        return (blank_of(first()), made)

    return lax.cond(section_index == 0, first_branch, second_branch)


def phase_one(section_id, packed, inputs, extents, views):
    middle, outward, height, breadth = section_shape(section_id)
    if section_id == 1:
        source = inputs[:, ::2, ::2, :]
        extents = extents // 2
    else:
        source = inputs
    pixel_mask, weighted, selector = layout(extents, views, height, breadth)
    weights = unpack_weights(packed, section_id)
    rows_in = source.reshape(-1, C0)
    first_z = jnp.dot(rows_in, weights[0], preferred_element_type=jnp.float32)
    if section_id == 1:
        side_z = jnp.dot(rows_in, weights[3], preferred_element_type=jnp.float32)
        first_z = jnp.concatenate([first_z, side_z], axis=1)
    shared = (widen_to(moments(first_z, weighted), M1 + C1), jnp.sum(weighted, axis=0))
    return (shared, (rows_in, first_z, pixel_mask, weighted, selector))


def phase_two(section_id, packed, norm_row, totals, counts, first):
    middle, outward, height, breadth = section_shape(section_id)
    rows_in, first_z, pixel_mask, weighted, selector = first
    weights = unpack_weights(packed, section_id)
    slices = norm_slices(norm_row, section_id)
    normed_one, scale_one = normalize(first_z, totals[:, :, : first_z.shape[1]], counts, selector)
    pre_one = normed_one[:, :middle] * slices[0][0] + slices[0][1]
    act_one = (silu_value(pre_one) * pixel_mask).astype(jnp.bfloat16)
    cols_two = patches(act_one.reshape(IMG_MB, height, breadth, middle))
    second_z = jnp.dot(cols_two, weights[1], preferred_element_type=jnp.float32)
    return (
        widen_to(moments(second_z, weighted), M1),
        (normed_one, scale_one, pre_one, cols_two, second_z),
    )


def phase_three(section_id, packed, norm_row, totals, counts, first, second):
    middle, outward, height, breadth = section_shape(section_id)
    rows_in, first_z, pixel_mask, weighted, selector = first
    second_z = second[4]
    weights = unpack_weights(packed, section_id)
    slices = norm_slices(norm_row, section_id)
    normed_two, scale_two = normalize(second_z, totals[:, :, :middle], counts, selector)
    pre_two = normed_two * slices[1][0] + slices[1][1]
    act_two = (silu_value(pre_two) * pixel_mask).astype(jnp.bfloat16)
    third_z = jnp.dot(act_two, weights[2], preferred_element_type=jnp.float32)
    return (
        widen_to(moments(third_z, weighted), C1),
        (normed_two, scale_two, pre_two, act_two, third_z),
    )


def finish(section_id, norm_row, totals, counts, first, second, third):
    middle, outward, height, breadth = section_shape(section_id)
    rows_in, first_z, pixel_mask, weighted, selector = first
    normed_one = second[0]
    slices = norm_slices(norm_row, section_id)
    normed_three, scale_three = normalize(third[4], totals[:, :, :outward], counts, selector)
    branch_out = normed_three * slices[2][0] + slices[2][1]
    if section_id == 1:
        residual = normed_one[:, middle:] * slices[3][0] + slices[3][1]
    else:
        residual = rows_in.astype(jnp.float32)
    pre_out = branch_out + residual
    result = (silu_value(pre_out) * pixel_mask).astype(jnp.bfloat16)
    if section_id == 0:
        shaped = result.reshape(IMG_MB, HB, WB, C0)
    else:
        shaped = result.reshape(IMG_MB, -1)
    return (normed_three, scale_three, pre_out, shaped)


def back_three(section_id, state, grad_out):
    middle, outward, height, breadth = section_shape(section_id)
    first, second, third, fourth, counts = state
    pixel_mask, weighted = (first[2], first[3])
    grad_pre = grad_out * silu_slope(fourth[2]) * pixel_mask
    sums_now = back_moments(grad_pre, fourth[0], weighted)
    if section_id == 1:
        sums_now = jnp.concatenate(
            [sums_now, back_moments(grad_pre, second[0][:, middle:], weighted)], axis=2
        )
    return (widen_to(sums_now, 2 * C1), grad_pre)


def back_two(section_id, packed, norm_row, back_totals, state, grad_pre):
    middle, outward, height, breadth = section_shape(section_id)
    first, second, third, fourth, counts = state
    rows_in, first_z, pixel_mask, weighted, selector = first
    weights = unpack_weights(packed, section_id)
    slices = norm_slices(norm_row, section_id)
    delta_three = norm_back(
        grad_pre,
        fourth[0],
        fourth[1],
        slices[2][0],
        back_totals[:, :, :outward],
        counts,
        selector,
        pixel_mask,
    ).astype(jnp.bfloat16)
    deltas = (delta_three,)
    if section_id == 1:
        delta_side = norm_back(
            grad_pre,
            second[0][:, middle:],
            second[1][:, middle:],
            slices[3][0],
            back_totals[:, :, outward : outward + C1],
            counts,
            selector,
            pixel_mask,
        ).astype(jnp.bfloat16)
        deltas = (delta_three, delta_side)
    grad_act = jnp.dot(delta_three, weights[2].T, preferred_element_type=jnp.float32)
    grad_two = grad_act * pixel_mask * silu_slope(third[2])
    return (widen_to(back_moments(grad_two, third[0], weighted), M1), (deltas, grad_two))


def back_one(section_id, packed, norm_row, back_totals, state, grad_two):
    middle, outward, height, breadth = section_shape(section_id)
    first, second, third, fourth, counts = state
    rows_in, first_z, pixel_mask, weighted, selector = first
    weights = unpack_weights(packed, section_id)
    slices = norm_slices(norm_row, section_id)
    delta_two = norm_back(
        grad_two,
        third[0],
        third[1],
        slices[1][0],
        back_totals[:, :, :middle],
        counts,
        selector,
        pixel_mask,
    ).astype(jnp.bfloat16)
    grad_cols = jnp.dot(delta_two, weights[1].T, preferred_element_type=jnp.float32)
    grad_act = unpatch(grad_cols, IMG_MB, height, breadth, middle)
    grad_one = grad_act * pixel_mask * silu_slope(second[2])
    return (
        widen_to(back_moments(grad_one, second[0][:, :middle], weighted), M1),
        (delta_two, grad_one),
    )


def back_zero(section_id, packed, norm_row, back_totals, state, grad_pre, deltas, grad_one):
    middle, outward, height, breadth = section_shape(section_id)
    first, second, third, fourth, counts = state
    rows_in, first_z, pixel_mask, weighted, selector = first
    weights = unpack_weights(packed, section_id)
    slices = norm_slices(norm_row, section_id)
    delta_one = norm_back(
        grad_one,
        second[0][:, :middle],
        second[1][:, :middle],
        slices[0][0],
        back_totals[:, :, :middle],
        counts,
        selector,
        pixel_mask,
    ).astype(jnp.bfloat16)
    grad_in = jnp.dot(delta_one, weights[0].T, preferred_element_type=jnp.float32)
    if section_id == 1:
        grad_in = grad_in + jnp.dot(deltas[1], weights[3].T, preferred_element_type=jnp.float32)
        spread_out = jnp.zeros((IMG_MB, HB, WB, C0), jnp.float32)
        spread_out = spread_out.at[:, ::2, ::2, :].set(
            grad_in.reshape(IMG_MB, HB // 2, WB // 2, C0)
        )
        result = spread_out.astype(jnp.bfloat16)
    else:
        result = (grad_in + grad_pre).astype(jnp.bfloat16).reshape(IMG_MB, -1)
    return (delta_one, result)


def weight_items(section_id, state, deltas, delta_two, delta_one):
    first, second, third, fourth, counts = state
    rows_in = first[0]
    pairs = [(rows_in, delta_one), (second[3], delta_two), (third[3], deltas[0])]
    if section_id == 1:
        pairs.append((rows_in, deltas[1]))
    return pairs


def weight_pass(item_list):
    pieces = []
    for piece_no in range(len(item_list[0])):
        left_rows = jnp.concatenate([entry[piece_no][0] for entry in item_list], axis=0)
        right_rows = jnp.concatenate([entry[piece_no][1] for entry in item_list], axis=0)
        product = lax.dot_general(
            left_rows, right_rows, (((0,), (0,)), ((), ())), preferred_element_type=jnp.float32
        )
        pieces.append(product.reshape(-1))
    joined = jnp.concatenate(pieces)
    return jnp.pad(joined, (0, P_SIZE - joined.shape[0]))


def map_norms(section_id, sums_three, sums_two, sums_one):
    middle, outward, height, breadth = section_shape(section_id)

    def gain_shift(piece):
        return jnp.stack([jnp.sum(piece[1], axis=0), jnp.sum(piece[0], axis=0)])

    parts = [
        gain_shift(sums_one[:, :, :middle]),
        gain_shift(sums_two[:, :, :middle]),
        gain_shift(sums_three[:, :, :outward]),
    ]
    if section_id == 1:
        parts.append(gain_shift(sums_three[:, :, outward : outward + C1]))
    joined = jnp.concatenate(parts, axis=1)
    return jnp.pad(joined, ((0, 0), (0, CN - joined.shape[1])))


def sync_moments(values):
    return lax.psum(values, "dp")


def sync_grads(values):
    return lax.psum(values, "dp")


def on_device(images, extents, views, params, norms, cotangent):
    section_index = lax.axis_index("pipe")
    packed = params[0]
    norm_row = norms[0]
    received = jnp.zeros((IMG_MB, HB, WB, C0), jnp.bfloat16)
    stored = {}
    behind_state = None
    items_ahead = {}
    items_behind = {}
    grad_rows = {}
    out_rows = {}
    sums_one = jnp.zeros((2, 2, M1), jnp.float32)
    sums_two = jnp.zeros((2, 2, M1), jnp.float32)
    sums_three = jnp.zeros((2, 2, 2 * C1), jnp.float32)
    for step_no in range(MB + 2):
        ahead_on = step_no < MB
        behind_on = 1 <= step_no <= MB
        back_on = step_no >= 2
        ahead_mb = min(step_no, MB - 1)
        behind_mb = min(max(step_no - 1, 0), MB - 1)
        return_mb = min(max(step_no - 2, 0), MB - 1)
        outgoing = jnp.zeros((IMG_MB, HB, WB, C0), jnp.bfloat16)
        if step_no <= MB:
            in_ahead = micro_slice(images, ahead_mb)
            ahead_one, behind_one = by_section(
                section_index,
                lambda: phase_one(
                    0,
                    packed,
                    in_ahead,
                    micro_slice(extents, ahead_mb),
                    micro_slice(views, ahead_mb),
                ),
                lambda: phase_one(
                    1,
                    packed,
                    received,
                    micro_slice(extents, behind_mb),
                    micro_slice(views, behind_mb),
                ),
                ahead_on,
                behind_on,
            )
            moment_sums = ahead_one[0][0] + behind_one[0][0]
            pixel_counts = ahead_one[0][1] + behind_one[0][1]
            totals, counts = lax.psum((moment_sums, pixel_counts), "dp")
            first_ahead, first_behind = (ahead_one[1], behind_one[1])
            ahead_two, behind_two = by_section(
                section_index,
                lambda: phase_two(0, packed, norm_row, totals, counts, first_ahead),
                lambda: phase_two(1, packed, norm_row, totals, counts, first_behind),
                ahead_on,
                behind_on,
            )
            totals_two = sync_moments(ahead_two[0] + behind_two[0])
            second_ahead, second_behind = (ahead_two[1], behind_two[1])
            ahead_three, behind_three = by_section(
                section_index,
                lambda: phase_three(
                    0, packed, norm_row, totals_two, counts, first_ahead, second_ahead
                ),
                lambda: phase_three(
                    1, packed, norm_row, totals_two, counts, first_behind, second_behind
                ),
                ahead_on,
                behind_on,
            )
            totals_three = sync_moments(ahead_three[0] + behind_three[0])
            third_ahead, third_behind = (ahead_three[1], behind_three[1])
            fourth_ahead, fourth_behind = by_section(
                section_index,
                lambda: finish(
                    0, norm_row, totals_three, counts, first_ahead, second_ahead, third_ahead
                ),
                lambda: finish(
                    1, norm_row, totals_three, counts, first_behind, second_behind, third_behind
                ),
                ahead_on,
                behind_on,
            )
            if ahead_on:
                stored[ahead_mb] = (first_ahead, second_ahead, third_ahead, fourth_ahead, counts)
                outgoing = fourth_ahead[3]
            if behind_on:
                behind_state = (first_behind, second_behind, third_behind, fourth_behind, counts)
                out_rows[behind_mb] = fourth_behind[3]
        if step_no >= 1:
            ahead_state = stored[return_mb]
            grad_ahead = received.astype(jnp.float32).reshape(-1, C0)
            grad_behind = micro_slice(cotangent, behind_mb).astype(jnp.float32).reshape(-1, C1)
            ahead_b3, behind_b3 = by_section(
                section_index,
                lambda: back_three(0, ahead_state, grad_ahead),
                lambda: back_three(1, behind_state, grad_behind),
                back_on,
                behind_on,
            )
            back_three_tot = sync_grads(ahead_b3[0] + behind_b3[0])
            ahead_b2, behind_b2 = by_section(
                section_index,
                lambda: back_two(0, packed, norm_row, back_three_tot, ahead_state, ahead_b3[1]),
                lambda: back_two(1, packed, norm_row, back_three_tot, behind_state, behind_b3[1]),
                back_on,
                behind_on,
            )
            back_two_tot = sync_grads(ahead_b2[0] + behind_b2[0])
            ahead_b1, behind_b1 = by_section(
                section_index,
                lambda: back_one(0, packed, norm_row, back_two_tot, ahead_state, ahead_b2[1][1]),
                lambda: back_one(1, packed, norm_row, back_two_tot, behind_state, behind_b2[1][1]),
                back_on,
                behind_on,
            )
            back_one_tot = sync_grads(ahead_b1[0] + behind_b1[0])
            ahead_b0, behind_b0 = by_section(
                section_index,
                lambda: back_zero(
                    0,
                    packed,
                    norm_row,
                    back_one_tot,
                    ahead_state,
                    ahead_b3[1],
                    ahead_b2[1][0],
                    ahead_b1[1][1],
                ),
                lambda: back_zero(
                    1,
                    packed,
                    norm_row,
                    back_one_tot,
                    behind_state,
                    behind_b3[1],
                    behind_b2[1][0],
                    behind_b1[1][1],
                ),
                back_on,
                behind_on,
            )
            sums_three = sums_three + back_three_tot
            sums_two = sums_two + back_two_tot
            sums_one = sums_one + back_one_tot
            now_ahead = weight_items(0, ahead_state, ahead_b2[1][0], ahead_b1[1][0], ahead_b0[0])
            now_behind = weight_items(
                1, behind_state, behind_b2[1][0], behind_b1[1][0], behind_b0[0]
            )
            if back_on:
                grad_rows[return_mb] = ahead_b0[1]
                items_ahead[return_mb] = now_ahead
            if behind_on:
                outgoing = outgoing + behind_b0[1]
                items_behind[behind_mb] = now_behind
        if step_no <= MB:
            received = from_behind(outgoing, "pipe", 1)
    flat_ahead, flat_behind = by_section(
        section_index,
        lambda: weight_pass([items_ahead[k] for k in range(MB)]),
        lambda: weight_pass([items_behind[k] for k in range(MB)]),
        True,
        True,
    )
    grad_shard = lax.psum_scatter(flat_ahead + flat_behind, "dp", scatter_dimension=0, tiled=True)
    weight_grads = lax.all_gather(for_sending(grad_shard), "dp", axis=0, tiled=True).astype(
        grad_shard.dtype
    )
    norm_ahead, norm_behind = by_section(
        section_index,
        lambda: map_norms(0, sums_three, sums_two, sums_one),
        lambda: map_norms(1, sums_three, sums_two, sums_one),
        True,
        True,
    )
    norm_grads = norm_ahead + norm_behind
    input_rows = jnp.concatenate([grad_rows[k] for k in range(MB)], axis=0)
    output_rows = jnp.concatenate([out_rows[k] for k in range(MB)], axis=0)
    output_rows = jnp.pad(output_rows, ((0, 0), (0, input_rows.shape[1] - output_rows.shape[1])))
    boundary = input_rows + output_rows
    return (boundary[None], weight_grads[None], norm_grads[None])


def solution(mesh):
    placed = (
        P("dp", None, None, None),
        P("dp", None),
        P("dp"),
        P("pipe", None),
        P("pipe", None, None),
        P("dp", None, None, None),
    )
    return jax.shard_map(
        on_device,
        mesh=mesh,
        in_specs=placed,
        out_specs=(P("pipe", "dp", None), P("pipe", None), P("pipe", None, None)),
        check_vma=False,
    )
```

profile of v0, /device:TPU:0, one launch (start us, length us, event | category | flops | bytes accessed | tf_op | source)
XLA Modules:
  0.0 4219.1 jit_solution(7657939749840536829)
XLA Ops:
  7.2 255.8 %reduce.200 = bf16[6029312]{0:T(1024)(128)(2,1)} reduce(bf16[1,6029312]{1,0:T(2,128)(2,1)} %param.237, bf16[]{:T(256)} %constant.3000), dimensions={0}, to_apply=%param.237.reduce_sub_computation | reduce | bytes 24117250 | tf_op args[3]
  274.0 78.7 %all-reduce.48 = (f32[2,2,2560]{2,1,0:T(2,128)S(1)}, f32[2]{0:T(128)S(1)}) all-reduce(f32[2,2,2560]{2,1,0:T(2,128)S(1)} %broadcast_add_fusion.2, f32[2]{0:T(128)S(1)} %broadcast_add_fusion.9), channel_id=1, replica_groups=mesh['pipe'=2,'dp'=16] {'dp'}, use_global_device_ids=true, to_apply=%region_3.4 | all-reduce | flops 10242 | bytes 81936 | tf_op jit(solution)/shard_map/psum | solution.py:431
  352.7 43.8 %conditional.43 = (f32[2,2,512]{2,1,0:T(2,128)S(1)}, f32[512,256]{0,1:T(8,128)S(1)}, f32[512,256]{0,1:T(8,128)S(1)}, f32[512,256]{0,1:T(8,128)S(1)}, bf16[512,23...) conditional(s32[]{:T(128)} %convert_element_type.573, () %tuple.682, (f32[2,2,2560]{2,1,0:T(2,128)S(1)}, ...), branch_computations={%region_5.6_spmd.clone, %region_6.7_spmd.clone} | conditional | flops 618015744 | bytes 35560708 | solution.py:165
  449.5 73.6 %psum.248 = f32[2,2,2048]{2,1,0:T(2,128)S(1)} all-reduce(f32[2,2,2048]{2,1,0:T(2,128)S(1)} %broadcast_add_fusion.3), channel_id=1, replica_groups=mesh['pipe'=2,'dp'=16] {'dp'}, use_global_device_ids=true, to_apply=%region_10.11 | all-reduce | flops 8192 | bytes 65536 | tf_op jit(solution)/shard_map/psum | solution.py:379
  547.4 72.4 %all-reduce.47 = (f32[2,2,2560]{2,1,0:T(2,128)}, f32[2]{0:T(128)S(1)}) all-reduce(f32[2,2,2560]{2,1,0:T(2,128)S(1)} %add.1466, f32[2]{0:T(128)S(1)} %add.1467), channel_id=1, replica_groups=mesh['pipe'=2,'dp'=16] {'dp'}, use_global_device_ids=true, to_apply=%region_17.18 | all-reduce | flops 10242 | bytes 81936 | tf_op jit(solution)/shard_map/psum | solution.py:431
  619.9 38.0 conditional.47
  716.7 74.2 %psum.252 = f32[2,2,2048]{2,1,0:T(2,128)} all-reduce(f32[2,2,2048]{2,1,0:T(2,128)} %add.1469), channel_id=1, replica_groups=mesh['pipe'=2,'dp'=16] {'dp'}, use_global_device_ids=true, to_apply=%region_24.25 | all-reduce | flops 8192 | bytes 65536 | tf_op jit(solution)/shard_map/psum | solution.py:379
  809.1 98.0 %all-reduce.56.cloned.1.call-done = f32[2,2,4096]{2,1,0:T(2,128)} async-done(((f32[2,2,4096]{2,1,0:T(2,128)}), f32[2,2,4096]{2,1,0:T(2,128)}) %all-reduce.56.cloned.1.call-update) | async-done | bytes 65552 | tf_op jit(solution)/shard_map/psum | solution.py:383
  907.5 40.9 psum.254
  989.1 104.5 %collective-permute-start.1 = (bf16[2,16,16,1024]{3,2,1,0:T(8,128)(2,1)S(1)}, bf16[2,16,16,1024]{3,2,1,0:T(8,128)(2,1)}, u32[]{:S(2)}, u32[]{:S(2)}) collective-permute-start(bf16[2,16,16,1024]{3,2,1,0:T(8,128)(2,1)S(1)} %add.1471), channel_id=1, source_target_pairs={{0,16},{16,0},{1,17},{17,1},{2,18},{18,2},{3,19},{19,3},{4,20},{20... | collective-permute-start | bytes 3145736 | tf_op jit(solution)/shard_map/ppermute | solution.py:25
  1107.6 74.0 %all-reduce.46 = (f32[2,2,2560]{2,1,0:T(2,128)}, f32[2]{0:T(128)S(1)}) all-reduce(f32[2,2,2560]{2,1,0:T(2,128)S(1)} %add.1472, f32[2]{0:T(128)S(1)} %add.1473), channel_id=1, replica_groups=mesh['pipe'=2,'dp'=16] {'dp'}, use_global_device_ids=true, to_apply=%region_44.45 | all-reduce | flops 10242 | bytes 81936 | tf_op jit(solution)/shard_map/psum | solution.py:431
  1278.5 74.2 %psum.259 = f32[2,2,2048]{2,1,0:T(2,128)} all-reduce(f32[2,2,2048]{2,1,0:T(2,128)} %add.1475), channel_id=1, replica_groups=mesh['pipe'=2,'dp'=16] {'dp'}, use_global_device_ids=true, to_apply=%region_51.52 | all-reduce | flops 8192 | bytes 65536 | tf_op jit(solution)/shard_map/psum | solution.py:379
  1383.3 97.9 %all-reduce.58.cloned.1.call-done = f32[2,2,4096]{2,1,0:T(2,128)} async-done(((f32[2,2,4096]{2,1,0:T(2,128)}), f32[2,2,4096]{2,1,0:T(2,128)}) %all-reduce.58.cloned.1.call-update) | async-done | bytes 65552 | tf_op jit(solution)/shard_map/psum | solution.py:383
  1518.3 40.9 psum.261
  1559.2 45.1 %conditional.60 = (f32[2,2,512]{2,1,0:T(2,128)S(1)}, bf16[512,256]{1,0:T(8,128)(2,1)}, f32[512,256]{1,0:T(8,128)}, f32[2,2,512]{2,1,0:T(2,128)S(1)}, bf16[128,512]{1,0:T(8,128)(2,1)}, /*index=5*/f32[128,512]{1,0:T(8,128)S(1)}) conditional(s32[]{:T(128)} %convert_element_type.573, (f32[128,1]{0,1:T(1,128)S(1)}, f32[128,512]{1,0:T(8,128)}, ...), branch_computations={%region_60.62_spmd, %region_62.64_spmd} | conditional | flops 619979776 | bytes 66252052 | solution.py:165
  1671.5 74.3 %all-reduce.45 = (f32[2,2,2560]{2,1,0:T(2,128)}, f32[2]{0:T(128)S(1)}) all-reduce(f32[2,2,2560]{2,1,0:T(2,128)S(1)} %add.1480, f32[2]{0:T(128)S(1)} %add.1481), channel_id=1, replica_groups=mesh['pipe'=2,'dp'=16] {'dp'}, use_global_device_ids=true, to_apply=%region_72.73 | all-reduce | flops 10242 | bytes 81936 | tf_op jit(solution)/shard_map/psum | solution.py:431
  1841.8 74.2 %psum.266 = f32[2,2,2048]{2,1,0:T(2,128)} all-reduce(f32[2,2,2048]{2,1,0:T(2,128)} %add.1483), channel_id=1, replica_groups=mesh['pipe'=2,'dp'=16] {'dp'}, use_global_device_ids=true, to_apply=%region_79.80 | all-reduce | flops 8192 | bytes 65536 | tf_op jit(solution)/shard_map/psum | solution.py:379
  1947.2 98.0 %all-reduce.60.cloned.1.call-done = f32[2,2,4096]{2,1,0:T(2,128)} async-done(((f32[2,2,4096]{2,1,0:T(2,128)}), f32[2,2,4096]{2,1,0:T(2,128)}) %all-reduce.60.cloned.1.call-update) | async-done | bytes 65552 | tf_op jit(solution)/shard_map/psum | solution.py:383
  2045.1 38.6 conditional.67
  2083.7 40.4 psum.268
  2124.1 57.7 %conditional.68 = (f32[2,2,512]{2,1,0:T(2,128)S(1)}, bf16[512,256]{1,0:T(8,128)(2,1)}, f32[512,256]{1,0:T(8,128)}, f32[2,2,512]{2,1,0:T(2,128)S(1)}, bf16[128,51...) conditional(s32[]{:T(128)} %convert_element_type.573, (f32[128,1]{0,1:T(1,128)S(1)}, f32[128,512]{1,0:T(8,128)}, ...), branch_computations={%region_88.90_spmd, %region_90.92_spmd} | conditional | flops 619979776 | bytes 62578892 | solution.py:165
  2234.5 73.7 %all-reduce.44 = (f32[2,2,2560]{2,1,0:T(2,128)S(1)}, f32[2]{0:T(128)S(1)}) all-reduce(f32[2,2,2560]{2,1,0:T(2,128)S(1)} %broadcast_add_fusion.1, f32[2]{0:T(128)S(1)} %broadcast_add_fusion.8), channel_id=1, replica_groups=mesh['pipe'=2,'dp'=16] {'dp'}, use_global_device_ids=true, to_apply=%region_99.100 | all-reduce | flops 10242 | bytes 81936 | tf_op jit(solution)/shard_map/psum | solution.py:431
  2349.0 73.6 %psum.273 = f32[2,2,2048]{2,1,0:T(2,128)S(1)} all-reduce(f32[2,2,2048]{2,1,0:T(2,128)S(1)} %get-tuple-element.3413), channel_id=1, replica_groups=mesh['pipe'=2,'dp'=16] {'dp'}, use_global_device_ids=true, to_apply=%region_106.107 | all-reduce | flops 8192 | bytes 65536 | tf_op jit(solution)/shard_map/psum | solution.py:379
  2441.1 137.8 %all-reduce.62.cloned.1.call-done = f32[2,2,4096]{2,1,0:T(2,128)} async-done(((f32[2,2,4096]{2,1,0:T(2,128)}), f32[2,2,4096]{2,1,0:T(2,128)}) %all-reduce.62.cloned.1.call-update) | async-done | bytes 65552 | tf_op jit(solution)/shard_map/psum | solution.py:383
  2614.3 41.0 psum.275
  2655.3 59.0 %conditional.76 = (f32[2,2,512]{2,1,0:T(2,128)S(1)}, bf16[512,256]{1,0:T(8,128)(2,1)}, f32[512,256]{1,0:T(8,128)}, f32[2,2,512]{2,1,0:T(2,128)S(1)}, bf16[128,51...) conditional(s32[]{:T(128)} %convert_element_type.573, (f32[128,1]{0,1:T(1,128)}, f32[128,512]{0,1:T(8,128)}, ...), branch_computations={%region_115.117_spmd, %region_117.119_spmd} | conditional | flops 619979776 | bytes 62061788 | solution.py:165
  2778.5 98.7 %all-reduce.64.cloned.1.call-done = f32[2,2,4096]{2,1,0:T(2,128)} async-done(((f32[2,2,4096]{2,1,0:T(2,128)}), f32[2,2,4096]{2,1,0:T(2,128)}) %all-reduce.64.cloned.1.call-update) | async-done | bytes 65552 | tf_op jit(solution)/shard_map/psum | solution.py:383
  2905.1 40.4 psum.278
  2946.3 40.0 conditional.80
  3040.7 78.2 %conditional.82 = (f32[6029312]{0:T(1024)}, f32[6029312]{0:T(1024)}) conditional(s32[]{:T(128)} %convert_element_type.573, (bf16[128,1024]{1,0:T(8,128)(2,1)S(1)}, bf16[128,1024]{1,0:T(8,128)(2,1)S(1)}, bf16[128,1024]{1,0:T(8,128)(2,1)}, bf16[128,1024]{1,0:T(8,128)(2,1)}, bf16[128,512]{0,1:T(8,128)(2,1)}, ...), branch_computations={%region_135.136_spmd, %region_136.137_spmd} | conditional | flops 6234046464 | bytes 197919344 | solution.py:165
  3143.5 898.5 %all-reduce.65 = bf16[6029312]{0:T(1024)(128)(2,1)} all-reduce(f32[6029312]{0:T(1024)} %add.1499), channel_id=2, replica_groups=mesh['pipe'=2,'dp'=16] {'dp'}, use_global_device_ids=true, to_apply=%region_137.138.clone | all-reduce | flops 6029312 | bytes 36175872
  4060.0 138.3 %all-gather.2.cloned.1.call-done = bf16[6029312]{0:T(1024)(128)(2,1)} async-done(((bf16[376832]{0:T(1024)(128)(2,1)}), bf16[6029312]{0:T(1024)(128)(2,1)}) %all-gather.2.cloned.1.call-update) | async-done | bytes 12058640 | tf_op jit(solution)/shard_map/all_gather | solution.py:548
  (1101 shorter events, 1737.1 us)
Async XLA Ops:
  7.2 899.9 %all-reduce.56.cloned.1.call-start = ((), (), s32[]{:S(2)}) async-start(), calls=%async_computation | async-start | bytes 131072 | tf_op jit(solution)/shard_map/psum | solution.py:383
  7.2 255.9 %copy-start.224 = (s32[8,2]{0,1:T(2,128)S(1)}, s32[8,2]{0,1:T(2,128)}, u32[]{:S(2)}) copy-start(s32[8,2]{0,1:T(2,128)} %param.235) | copy-start | bytes 196
  7.2 255.9 %copy-start.241 = (s32[8]{0:T(128)S(1)}, s32[8]{0:T(128)}, u32[]{:S(2)}) copy-start(s32[8]{0:T(128)} %param.236) | copy-start | bytes 100
  273.9 249.2 %copy-start.6 = (f32[512,2]{1,0:T(8,128)}, f32[512,2]{1,0:T(8,128)S(1)}, u32[]{:S(2)}) copy-start(f32[512,2]{1,0:T(8,128)S(1)} %get-tuple-element.3108) | copy-start | bytes 12292
  274.0 249.2 %copy-start.222 = (f32[512,1]{0,1:T(1,128)}, f32[512,1]{0,1:T(1,128)S(1)}, u32[]{:S(2)}) copy-start(f32[512,1]{0,1:T(1,128)S(1)} %get-tuple-element.3110) | copy-start | bytes 6148
  352.7 170.5 %copy-start.227 = (f32[2]{0:T(128)}, f32[2]{0:T(128)S(1)}, u32[]{:S(2)}) copy-start(f32[2]{0:T(128)S(1)} %get-tuple-element.5643) | copy-start | bytes 28
  532.6 3.4 collective-permute-start
  547.4 243.5 %copy-start = (f32[512,2]{1,0:T(8,128)}, f32[512,2]{1,0:T(8,128)S(1)}, u32[]{:S(2)}) copy-start(f32[512,2]{1,0:T(8,128)S(1)} %get-tuple-element.3128) | copy-start | bytes 12292
  547.4 243.5 %copy-start.33 = (f32[512,1]{1,0:T(8,128)}, f32[512,1]{1,0:T(8,128)S(1)}, u32[]{:S(2)}) copy-start(f32[512,1]{1,0:T(8,128)S(1)} %get-tuple-element.3130) | copy-start | bytes 6148
  619.9 367.4 %copy-start.195 = (f32[2]{0:T(128)}, f32[2]{0:T(128)S(1)}, u32[]{:S(2)}) copy-start(f32[2]{0:T(128)S(1)} %get-tuple-element.5641) | copy-start | bytes 28
  809.1 672.2 %all-reduce.58.cloned.1.call-start = ((), (), s32[]{:S(2)}) async-start(), calls=%async_computation.1 | async-start | bytes 131072 | tf_op jit(solution)/shard_map/psum | solution.py:383
  989.1 107.0 %collective-permute-start.1 = (bf16[2,16,16,1024]{3,2,1,0:T(8,128)(2,1)S(1)}, bf16[2,16,16,1024]{3,2,1,0:T(8,128)(2,1)}, u32[]{:S(2)}, u32[]{:S(2)}) collective-permute-start(bf16[2,16,16,1024]{3,2,1,0:T(8,128)(2,1)S(1)} %add.1471), channel_id=1, source_target_pairs={{0,16},{16,0},{1,17},{17,1},{2,18},{18,2},{3,19},{19,3},{4,20},{20... | collective-permute-start | bytes 3145736 | tf_op jit(solution)/shard_map/ppermute | solution.py:25
  1107.5 245.1 %copy-start.2 = (f32[512,2]{1,0:T(8,128)}, f32[512,2]{1,0:T(8,128)S(1)}, u32[]{:S(2)}) copy-start(f32[512,2]{1,0:T(8,128)S(1)} %get-tuple-element.3168) | copy-start | bytes 12292
  1107.5 245.1 %copy-start.35 = (f32[512,1]{1,0:T(8,128)}, f32[512,1]{1,0:T(8,128)S(1)}, u32[]{:S(2)}) copy-start(f32[512,1]{1,0:T(8,128)S(1)} %get-tuple-element.3170) | copy-start | bytes 6148
  1107.6 245.1 %copy-start.229 = (f32[128,1]{0,1:T(1,128)}, f32[128,1]{0,1:T(1,128)S(1)}, u32[]{:S(2)}) copy-start(f32[128,1]{0,1:T(1,128)S(1)} %get-tuple-element.3160) | copy-start | bytes 1540
  1181.6 460.5 %copy-start.197 = (f32[2]{0:T(128)}, f32[2]{0:T(128)S(1)}, u32[]{:S(2)}) copy-start(f32[2]{0:T(128)S(1)} %get-tuple-element.5639) | copy-start | bytes 28
  1277.0 204.3 %copy-start.96 = (f32[128,512]{1,0:T(8,128)}, f32[128,512]{1,0:T(8,128)S(1)}, u32[]{:S(2)}) copy-start(f32[128,512]{1,0:T(8,128)S(1)} %get-tuple-element.3193) | copy-start | bytes 786436
  1383.3 661.8 %all-reduce.60.cloned.1.call-start = ((), (), s32[]{:S(2)}) async-start(), calls=%async_computation.2 | async-start | bytes 131072 | tf_op jit(solution)/shard_map/psum | solution.py:383
  1654.9 4.8 collective-permute-start.2
  1671.4 244.5 %copy-start.4 = (f32[512,2]{1,0:T(8,128)}, f32[512,2]{1,0:T(8,128)S(1)}, u32[]{:S(2)}) copy-start(f32[512,2]{1,0:T(8,128)S(1)} %get-tuple-element.3223) | copy-start | bytes 12292
  1671.4 244.5 %copy-start.37 = (f32[512,1]{1,0:T(8,128)}, f32[512,1]{1,0:T(8,128)S(1)}, u32[]{:S(2)}) copy-start(f32[512,1]{1,0:T(8,128)S(1)} %get-tuple-element.3225) | copy-start | bytes 6148
  1947.1 631.8 %all-reduce.62.cloned.1.call-start = ((), (), s32[]{:S(2)}) async-start(), calls=%async_computation.3 | async-start | bytes 131072 | tf_op jit(solution)/shard_map/psum | solution.py:383
  2231.1 2.9 collective-permute-start.3
  2234.5 344.4 %copy-start.234 = (f32[128,1]{0,1:T(1,128)}, f32[128,1]{0,1:T(1,128)S(1)}, u32[]{:S(2)}) copy-start(f32[128,1]{0,1:T(1,128)S(1)} %get-tuple-element.3270) | copy-start | bytes 1540
  2308.3 270.6 %copy-start.219 = (f32[2]{0:T(128)}, f32[2]{0:T(128)S(1)}, u32[]{:S(2)}) copy-start(f32[2]{0:T(128)S(1)} %get-tuple-element.5635) | copy-start | bytes 28
  2349.0 229.9 %copy-start.159 = (f32[128,512]{0,1:T(8,128)}, f32[128,512]{0,1:T(8,128)S(1)}, u32[]{:S(2)}) copy-start(f32[128,512]{0,1:T(8,128)S(1)} %get-tuple-element.3414) | copy-start | bytes 786436
  2429.4 149.4 %copy-start.3 = (f32[512,2]{1,0:T(8,128)S(1)}, f32[512,2]{1,0:T(8,128)}, u32[]{:S(2)}) copy-start(f32[512,2]{1,0:T(8,128)} %copy-done.2) | copy-start | bytes 12292
  2429.4 149.4 %copy-start.198 = (f32[2]{0:T(128)S(1)}, f32[2]{0:T(128)}, u32[]{:S(2)}) copy-start(f32[2]{0:T(128)} %copy-done.197) | copy-start | bytes 28
  2441.1 436.1 %all-reduce.64.cloned.1.call-start = ((), (), s32[]{:S(2)}) async-start(), calls=%async_computation.4 | async-start | bytes 131072 | tf_op jit(solution)/shard_map/psum | solution.py:383
  2763.0 2.7 collective-permute-start.4
  2777.3 1421.0 %all-gather.2.cloned.1.call-start = ((), (), s32[]{:S(2)}) async-start(), calls=%async_computation.5 | async-start | bytes 12812288 | tf_op jit(solution)/shard_map/all_gather | solution.py:548
  3143.5 901.4 %copy-start.110 = (bf16[2,131072]{1,0:T(2,128)(2,1)S(1)}, bf16[2,131072]{1,0:T(2,128)(2,1)}, u32[]{:S(2)}) copy-start(bf16[2,131072]{1,0:T(2,128)(2,1)} %copy-done.109) | copy-start | bytes 1572868
  (139 other events, 3659.8 us)
Sparse Core Ops, SparseCore 0:
  809.2 97.8 all-reduce.55
  1383.4 97.8 all-reduce.57
  1947.2 97.8 all-reduce.59
  2441.2 137.6 all-reduce.61
  2777.4 99.7 all-reduce.63
  4044.3 153.9 all-gather.1
where the time goes:
time: 4240 us; the launch traced here: 4220 us
  blocking collectives  2220 us (52%)
  waiting for transfers between devices  679 us (16%)
  other arithmetic  451 us (11%)
  local copies, waits for them, and re-layouts  401 us (9%)
  matrix products  304 us (7%)
  starting transfers between devices  107 us (3%)
    unnamed x1, blocking collectives  898 us
    psum x10, blocking collectives, sync_moments(): return lax.psum(values, 'dp')  557 us
    psum x5, waiting for transfers between devices, sync_grads(): return lax.psum(values, 'dp')  530 us
    psum x10, blocking collectives, sync_grads(): return lax.psum(values, 'dp')  391 us
    psum x5, blocking collectives, on_device(): totals, counts = lax.psum((moment_sums, pixel_counts), 'dp')  373 us
    unnamed x1, other arithmetic  256 us
    another operation x206, local copies, waits for them, and re-layouts  142 us
    all_gather x1, waiting for transfers between devices, on_device(): lax.all_gather(for_sending(grad_shard), 'dp', axis=0, tiled=True)  138 us
  transfers between devices with their start and end apart: 11, of which 10 were waited for; matrix products, arithmetic and copies ran while one was open for 0% of the time, Pallas kernels for 0%

commit v1 on v0

v1 whole, which is shorter than its diff:
```python
import functools

import jax
import jax.numpy as jnp
from jax import lax
from jax.experimental import pallas as pl
from jax.experimental.pallas import tpu as pltpu
from jax.sharding import PartitionSpec as P

C0 = 1024
M0 = 256
M1 = 512
C1 = 2048
HB = 16
WB = 16
IMG_MB = 2
MB = 4
P_SIZE = 6029312
CN = 5120
SLOTS = 4
PIX0 = 256
PIX1 = 64
EPSILON = 1e-05
MIB = 1 << 20

F32 = jnp.float32
BF16 = jnp.bfloat16


def shape_of(dims, kind):
    return jax.ShapeDtypeStruct(dims, kind)


def dot_nn(left, right):
    return lax.dot_general(left, right, (((1,), (0,)), ((), ())), preferred_element_type=F32)


def dot_nt(left, right):
    return lax.dot_general(left, right, (((1,), (1,)), ((), ())), preferred_element_type=F32)


def over_lanes(column, width):
    return jnp.concatenate([column] * (width // 128), axis=1)


def pixel_mask(high, wide, breadth, rows):
    index = lax.broadcasted_iota(jnp.int32, (rows, 128), 0)
    shift = breadth.bit_length() - 1
    inside = ((index >> shift) < high) & ((index & (breadth - 1)) < wide)
    return jnp.where(inside, 1.0, 0.0).astype(F32)


def column_of(breadth, rows, width):
    return lax.broadcasted_iota(jnp.int32, (rows, width), 0) & (breadth - 1)


def sigmoid(values):
    return 1.0 / (1.0 + jnp.exp(-values))


def silu(values):
    return values * sigmoid(values)


def slope(values):
    sig = sigmoid(values)
    return sig * (1.0 + values * (1.0 - sig))


def row_at(table, row):
    if isinstance(row, int):
        return table[row : row + 1, :]
    rows = lax.broadcasted_iota(jnp.int32, table.shape, 0)
    return jnp.sum(jnp.where(rows == row, table, 0.0), axis=0, keepdims=True)


def put_rows(ref, slot, first, second):
    if isinstance(slot, int):
        ref[2 * slot : 2 * slot + 1, :] = first
        ref[2 * slot + 1 : 2 * slot + 2, :] = second
        return
    rows = lax.broadcasted_iota(jnp.int32, ref.shape, 0)
    kept = jnp.where(rows == 2 * slot, first, ref[...])
    ref[...] = jnp.where(rows == 2 * slot + 1, second, kept)


def total_rows(values):
    return jnp.sum(values, axis=0, keepdims=True)


def mean_scale(table, slot, count):
    mean = row_at(table, 2 * slot) / count
    spread = row_at(table, 2 * slot + 1) / count - mean * mean
    return mean, lax.rsqrt(spread + EPSILON)


def back_means(table, slot, count):
    return row_at(table, 2 * slot) / count, row_at(table, 2 * slot + 1) / count


def count_of(table, slot):
    return row_at(table, 2 * slot)[:, M0 : M0 + 1]


def side_columns(values, breadth):
    rows, width = values.shape
    column = column_of(breadth, rows, width)
    left = jnp.where(column == 0, 0.0, pltpu.roll(values, 1, 0))
    right = jnp.where(column == breadth - 1, 0.0, pltpu.roll(values, rows - 1, 0))
    return left, right


def later_rows(values, step, height, breadth):
    if step == 0:
        return values
    rows, width = values.shape
    images = values.reshape(rows // (height * breadth), height * breadth, width)
    gap = jnp.zeros((images.shape[0], breadth, width), values.dtype)
    if step > 0:
        moved = jnp.concatenate([gap, images[:, :-breadth]], axis=1)
    else:
        moved = jnp.concatenate([images[:, breadth:], gap], axis=1)
    return moved.reshape(rows, width)


def even_picker():
    row = lax.broadcasted_iota(jnp.int32, (PIX1, PIX0), 0)
    col = lax.broadcasted_iota(jnp.int32, (PIX1, PIX0), 1)
    return jnp.where(col == 32 * (row >> 3) + 2 * (row & 7), 1.0, 0.0).astype(BF16)


def even_placer():
    row = lax.broadcasted_iota(jnp.int32, (PIX0, PIX1), 0)
    col = lax.broadcasted_iota(jnp.int32, (PIX0, PIX1), 1)
    return jnp.where(row == 32 * (col >> 3) + 2 * (col & 7), 1.0, 0.0).astype(BF16)


def placed(values):
    placer = even_placer()
    high = values.astype(BF16)
    rest = (values - high.astype(F32)).astype(BF16)
    return dot_nn(placer, high) + dot_nn(placer, rest)


def call(body, outs, grid, in_specs, out_specs, scratch=(), limit=40):
    return pl.pallas_call(
        body,
        out_shape=outs,
        grid_spec=pltpu.PrefetchScalarGridSpec(
            num_scalar_prefetch=1,
            grid=grid,
            in_specs=in_specs,
            out_specs=out_specs,
            scratch_shapes=list(scratch),
        ),
        compiler_params=pltpu.CompilerParams(vmem_limit_bytes=limit * MIB),
    )


def full(*dims):
    return pl.BlockSpec(dims, lambda *_: (0,) * len(dims))


def per_slot(*dims):
    return pl.BlockSpec((1,) + dims, lambda s, meta: (s,) + (0,) * len(dims))


def per_image(*dims):
    return pl.BlockSpec((1,) + dims, lambda s, meta: (meta[s],) + (0,) * len(dims))


def slot_mask0(meta, slot):
    return pixel_mask(meta[SLOTS + slot], meta[2 * SLOTS + slot], WB, PIX0)


def slot_mask1(meta, slot):
    return pixel_mask(meta[SLOTS + slot] >> 1, meta[2 * SLOTS + slot] >> 1, WB // 2, PIX1)


def front_one(meta, x_ref, w_ref, z_ref, st_ref):
    slot = pl.program_id(0)
    z = dot_nn(x_ref[0].reshape(PIX0, C0), w_ref[...])
    z_ref[0] = z
    zm = z * over_lanes(slot_mask0(meta, slot), M0)
    count = (meta[SLOTS + slot] * meta[2 * SLOTS + slot]).astype(F32)
    extra = jnp.full((1, 128), 1.0, F32) * count
    put_rows(
        st_ref,
        slot,
        jnp.concatenate([total_rows(zm), extra], axis=1),
        jnp.concatenate([total_rows(zm * z), extra], axis=1),
    )


def front_two(meta, r_ref, z_ref, n_ref, w_ref, tot_ref, act_ref, z2_ref, st_ref):
    slot = pl.program_id(0)

    @pl.when(slot == 0)
    def _():
        tot_ref[...] = jnp.sum(r_ref[...], axis=0)

    table = tot_ref[...]
    count = count_of(table, slot)
    mean, scale = mean_scale(table[:, :M0], slot, count)
    mask = over_lanes(slot_mask0(meta, slot), M0)
    pre = (z_ref[0] - mean) * scale * n_ref[0:1, :M0] + n_ref[1:2, :M0]
    act = silu(pre) * mask
    left, right = side_columns(act, WB)
    act_ref[0, 0:WB, :] = jnp.zeros((WB, 3 * M0), BF16)
    act_ref[0, WB + PIX0 : 2 * WB + PIX0, :] = jnp.zeros((WB, 3 * M0), BF16)
    act_ref[0, WB : WB + PIX0, :] = jnp.concatenate([left, act, right], axis=1).astype(BF16)
    z2 = dot_nn(act_ref[0, 0:PIX0, :], w_ref[0 : 3 * M0, :])
    z2 = z2 + dot_nn(act_ref[0, WB : WB + PIX0, :], w_ref[3 * M0 : 6 * M0, :])
    z2 = z2 + dot_nn(act_ref[0, 2 * WB : 2 * WB + PIX0, :], w_ref[6 * M0 :, :])
    z2_ref[0] = z2
    zm = z2 * mask
    put_rows(st_ref, slot, total_rows(zm), total_rows(zm * z2))


def front_three(meta, r_ref, tot_ref, z2_ref, n_ref, w_ref, tot2_ref, a2_ref, st_ref):
    slot = pl.program_id(0)

    @pl.when(slot == 0)
    def _():
        tot2_ref[...] = jnp.sum(r_ref[...], axis=0)

    count = count_of(tot_ref[...], slot)
    mean, scale = mean_scale(tot2_ref[...], slot, count)
    pre = (z2_ref[0] - mean) * scale * n_ref[0:1, M0 : 2 * M0] + n_ref[1:2, M0 : 2 * M0]
    act = (silu(pre) * over_lanes(slot_mask0(meta, slot), M0)).astype(BF16)
    a2_ref[0] = act
    z3 = dot_nn(act, w_ref[...])
    put_rows(st_ref, slot, total_rows(z3), total_rows(z3 * z3))


def join(
    meta, tot3_ref, tot_ref, a2_ref, x_ref, n_ref, w3_ref, w1_ref, ws_ref,
    s_ref, p_ref, z3_ref, z1_ref, zs_ref, st_ref, sts_ref,
):
    step = pl.program_id(0)

    @pl.when(step < SLOTS)
    def _():
        count = count_of(tot_ref[...], step)
        mean, scale = mean_scale(tot3_ref[...], step, count)
        picker = even_picker()
        act = dot_nn(picker, a2_ref[0]).astype(BF16)
        z3 = dot_nn(act, w3_ref[...])
        here = pl.ds(pl.multiple_of(step * PIX1, PIX1), PIX1)
        z3_ref[here, :] = z3
        pre = (z3 - mean) * scale * n_ref[0:1, 2 * M0 : 2 * M0 + C0]
        pre = pre + n_ref[1:2, 2 * M0 : 2 * M0 + C0]
        pre = pre + dot_nn(picker, x_ref[0].reshape(PIX0, C0))
        p_ref[here, :] = pre
        s_ref[here, :] = (silu(pre) * over_lanes(slot_mask1(meta, step), C0)).astype(BF16)

    @pl.when(step == SLOTS)
    def _():
        z1 = dot_nn(s_ref[...], w1_ref[...])
        z1_ref[...] = z1
        for slot in range(SLOTS):
            part = z1[slot * PIX1 : (slot + 1) * PIX1]
            put_rows(st_ref, slot, total_rows(part), total_rows(part * part))

    @pl.when(step >= SLOTS)
    def _():
        zs = dot_nn(s_ref[...], ws_ref[...])
        zs_ref[...] = zs
        for slot in range(SLOTS):
            part = zs[slot * PIX1 : (slot + 1) * PIX1]
            put_rows(sts_ref, slot, total_rows(part), total_rows(part * part))


def by_slot(pieces):
    return jnp.concatenate(pieces, axis=0)


def normed_slots(values, table, counts, width):
    pieces = []
    for slot in range(SLOTS):
        mean, scale = mean_scale(table, slot, counts[slot])
        pieces.append((values[slot * PIX1 : (slot + 1) * PIX1] - mean) * scale)
    return by_slot(pieces)


def counts1(tot_ref):
    table = tot_ref[...]
    return [count_of(table, slot) * 0.25 for slot in range(SLOTS)]


def mask1_all(meta, width):
    return over_lanes(by_slot([slot_mask1(meta, slot) for slot in range(SLOTS)]), width)


def slot_sums(st_ref, first, second):
    for slot in range(SLOTS):
        here = slice(slot * PIX1, (slot + 1) * PIX1)
        put_rows(st_ref, slot, total_rows(first[here]), total_rows(second[here]))


def mid_one(meta, r_ref, tot_ref, z1_ref, n_ref, w_ref, tot4_ref, act_ref, z2_ref, st_ref):
    tot4_ref[...] = jnp.sum(r_ref[...], axis=0)
    counts = counts1(tot_ref)
    mask = mask1_all(meta, M1)
    pre = normed_slots(z1_ref[...], tot4_ref[...], counts, M1) * n_ref[0:1, :M1] + n_ref[1:2, :M1]
    act = silu(pre) * mask
    left, right = side_columns(act, WB // 2)
    wide = jnp.concatenate([left, act, right], axis=1).astype(BF16)
    act_ref[...] = wide
    z2 = dot_nn(wide, w_ref[3 * M1 : 6 * M1, :])
    z2 = z2 + later_rows(dot_nn(wide, w_ref[0 : 3 * M1, :]), 1, HB // 2, WB // 2)
    z2 = z2 + later_rows(dot_nn(wide, w_ref[6 * M1 :, :]), -1, HB // 2, WB // 2)
    z2_ref[...] = z2
    zm = z2 * mask
    slot_sums(st_ref, zm, zm * z2)


def mid_two(meta, r_ref, tot_ref, z2_ref, n_ref, w_ref, tot5_ref, a2_ref, z3_ref, st_ref):
    tot5_ref[...] = jnp.sum(r_ref[...], axis=0)
    counts = counts1(tot_ref)
    pre = normed_slots(z2_ref[...], tot5_ref[...], counts, M1)
    pre = pre * n_ref[0:1, M1 : 2 * M1] + n_ref[1:2, M1 : 2 * M1]
    act = (silu(pre) * mask1_all(meta, M1)).astype(BF16)
    a2_ref[...] = act
    z3 = dot_nn(act, w_ref[...])
    z3_ref[...] = z3
    slot_sums(st_ref, z3, z3 * z3)


def turn(
    meta, tot6_ref, tots_ref, tot_ref, z3_ref, zs_ref, n_ref, cot_ref,
    y_ref, g_ref, st_ref, sts_ref,
):
    slot = pl.program_id(0)
    count = count_of(tot_ref[...], slot) * 0.25
    mask = over_lanes(slot_mask1(meta, slot), C1)
    mean, scale = mean_scale(tot6_ref[...], slot, count)
    normed = (z3_ref[0] - mean) * scale
    mean_s, scale_s = mean_scale(tots_ref[...], slot, count)
    normed_s = (zs_ref[0] - mean_s) * scale_s
    at3, ats = 2 * M1, 2 * M1 + C1
    pre = normed * n_ref[0:1, at3:ats] + n_ref[1:2, at3:ats]
    pre = pre + (normed_s * n_ref[0:1, ats : ats + C1] + n_ref[1:2, ats : ats + C1])
    sig = sigmoid(pre)
    y_ref[0] = (pre * sig * mask).astype(BF16).reshape(HB // 2, WB // 2, C1)
    grad = cot_ref[0].reshape(PIX1, C1).astype(F32) * (sig * (1.0 + pre * (1.0 - sig))) * mask
    g_ref[0] = grad
    put_rows(st_ref, slot, total_rows(grad), total_rows(grad * normed))
    put_rows(sts_ref, slot, total_rows(grad), total_rows(grad * normed_s))


def norm_back_slots(grad, normed, scales, gain, table, counts, mask):
    pieces = []
    for slot in range(SLOTS):
        here = slice(slot * PIX1, (slot + 1) * PIX1)
        first, second = back_means(table, slot, counts[slot])
        pieces.append(
            mask[here] * scales[slot] * gain * (grad[here] - first - normed[here] * second)
        )
    return by_slot(pieces).astype(BF16)


def scales_of(table, counts):
    return [mean_scale(table, slot, counts[slot])[1] for slot in range(SLOTS)]


def back_one(
    meta, tot7_ref, tot6_ref, tot5_ref, tot_ref, z3_ref, g_ref, z2_ref, n_ref, w_ref,
    d3_ref, g2_ref, st_ref,
):
    counts = counts1(tot_ref)
    mask = mask1_all(meta, C1)
    normed = normed_slots(z3_ref[...], tot6_ref[...], counts, C1)
    d3 = norm_back_slots(
        g_ref[...], normed, scales_of(tot6_ref[...], counts), n_ref[0:1, 2 * M1 : 2 * M1 + C1],
        tot7_ref[...], counts, mask,
    )
    d3_ref[...] = d3
    normed2 = normed_slots(z2_ref[...], tot5_ref[...], counts, M1)
    pre2 = normed2 * n_ref[0:1, M1 : 2 * M1] + n_ref[1:2, M1 : 2 * M1]
    g2 = dot_nt(d3, w_ref[...]) * mask[:, :M1] * slope(pre2)
    g2_ref[...] = g2
    slot_sums(st_ref, g2, g2 * normed2)


def back_two(
    meta, r_ref, tot5_ref, tot4_ref, tot_ref, z2_ref, g2_ref, z1_ref, n_ref, w_ref,
    tot8_ref, d2_ref, g1_ref, st_ref,
):
    tot8_ref[...] = jnp.sum(r_ref[...], axis=0)
    counts = counts1(tot_ref)
    mask = mask1_all(meta, M1)
    normed = normed_slots(z2_ref[...], tot5_ref[...], counts, M1)
    d2 = norm_back_slots(
        g2_ref[...], normed, scales_of(tot5_ref[...], counts), n_ref[0:1, M1 : 2 * M1],
        tot8_ref[...], counts, mask,
    )
    d2_ref[...] = d2
    wide = dot_nt(d2, w_ref[3 * M1 : 6 * M1, :])
    wide = wide + later_rows(dot_nt(d2, w_ref[0 : 3 * M1, :]), -1, HB // 2, WB // 2)
    wide = wide + later_rows(dot_nt(d2, w_ref[6 * M1 :, :]), 1, HB // 2, WB // 2)
    left, _ = side_columns(wide[:, 2 * M1 :], WB // 2)
    _, right = side_columns(wide[:, :M1], WB // 2)
    normed1 = normed_slots(z1_ref[...], tot4_ref[...], counts, M1)
    pre1 = normed1 * n_ref[0:1, :M1] + n_ref[1:2, :M1]
    g1 = (wide[:, M1 : 2 * M1] + left + right) * mask * slope(pre1)
    g1_ref[...] = g1
    slot_sums(st_ref, g1, g1 * normed1)


def back_three(
    meta, r_ref, tot4_ref, tot_ref, z1_ref, g1_ref, totg_ref, tots_ref, zs_ref, g_ref,
    tot3_ref, p_ref, z3_ref, n0_ref, n_ref, w1_ref, ws_ref,
    tot9_ref, d1_ref, ds_ref, g0_ref, st_ref,
):
    tot9_ref[...] = jnp.sum(r_ref[...], axis=0)
    counts = counts1(tot_ref)
    mask = mask1_all(meta, C1)
    normed = normed_slots(z1_ref[...], tot4_ref[...], counts, M1)
    d1 = norm_back_slots(
        g1_ref[...], normed, scales_of(tot4_ref[...], counts), n_ref[0:1, :M1],
        tot9_ref[...], counts, mask[:, :M1],
    )
    d1_ref[...] = d1
    normed_s = normed_slots(zs_ref[...], tots_ref[...], counts, C1)
    ats = 2 * M1 + C1
    ds = norm_back_slots(
        g_ref[...], normed_s, scales_of(tots_ref[...], counts), n_ref[0:1, ats : ats + C1],
        totg_ref[...], counts, mask,
    )
    ds_ref[...] = ds
    grad = dot_nt(d1, w1_ref[...]) + dot_nt(ds, ws_ref[...])
    grad = grad.astype(BF16).astype(F32)
    g0 = grad * slope(p_ref[...]) * mask[:, :C0]
    g0_ref[...] = g0
    counts0 = [count * 4.0 for count in counts]
    normed3 = normed_slots(z3_ref[...], tot3_ref[...], counts0, C0)
    slot_sums(st_ref, g0, g0 * normed3)


def norm_back(grad, normed, scale, gain, table, slot, count, mask):
    first, second = back_means(table, slot, count)
    return (mask * scale * gain * (grad - first - normed * second)).astype(BF16)


def last_one(
    meta, tot10_ref, tot3_ref, tot2_ref, tot_ref, a2_ref, g0_ref, z2_ref, n_ref, w_ref,
    d3_ref, g2_ref, st_ref,
):
    slot = pl.program_id(0)
    count = count_of(tot_ref[...], slot)
    mask = over_lanes(slot_mask0(meta, slot), C0)
    mean, scale = mean_scale(tot3_ref[...], slot, count)
    normed = (dot_nn(a2_ref[0], w_ref[...]) - mean) * scale
    grad = placed(g0_ref[0])
    d3 = norm_back(
        grad, normed, scale, n_ref[0:1, 2 * M0 : 2 * M0 + C0], tot10_ref[...], slot, count, mask
    )
    d3_ref[0] = d3
    mean2, scale2 = mean_scale(tot2_ref[...], slot, count)
    normed2 = (z2_ref[0] - mean2) * scale2
    pre2 = normed2 * n_ref[0:1, M0 : 2 * M0] + n_ref[1:2, M0 : 2 * M0]
    g2 = dot_nt(d3, w_ref[...]) * mask[:, :M0] * slope(pre2)
    g2_ref[0] = g2
    put_rows(st_ref, slot, total_rows(g2), total_rows(g2 * normed2))


def last_two(
    meta, r_ref, tot2_ref, tot_ref, z2_ref, g2_ref, z1_ref, n_ref, w_ref,
    tot11_ref, d2_ref, g1_ref, st_ref,
):
    slot = pl.program_id(0)

    @pl.when(slot == 0)
    def _():
        tot11_ref[...] = jnp.sum(r_ref[...], axis=0)

    table = tot_ref[...]
    count = count_of(table, slot)
    mask = over_lanes(slot_mask0(meta, slot), M0)
    mean2, scale2 = mean_scale(tot2_ref[...], slot, count)
    normed2 = (z2_ref[0] - mean2) * scale2
    d2 = norm_back(
        g2_ref[0], normed2, scale2, n_ref[0:1, M0 : 2 * M0], tot11_ref[...], slot, count, mask
    )
    d2_ref[0] = d2
    wide = dot_nt(d2, w_ref[3 * M0 : 6 * M0, :])
    wide = wide + later_rows(dot_nt(d2, w_ref[0 : 3 * M0, :]), -1, HB, WB)
    wide = wide + later_rows(dot_nt(d2, w_ref[6 * M0 :, :]), 1, HB, WB)
    left, _ = side_columns(wide[:, 2 * M0 :], WB)
    _, right = side_columns(wide[:, :M0], WB)
    mean1, scale1 = mean_scale(table[:, :M0], slot, count)
    normed1 = (z1_ref[0] - mean1) * scale1
    pre1 = normed1 * n_ref[0:1, :M0] + n_ref[1:2, :M0]
    g1 = (wide[:, M0 : 2 * M0] + left + right) * mask * slope(pre1)
    g1_ref[0] = g1
    put_rows(st_ref, slot, total_rows(g1), total_rows(g1 * normed1))


def last_three(meta, r_ref, tot_ref, z1_ref, g1_ref, g0_ref, n_ref, w_ref, tot12_ref, d1_ref, gx_ref):
    slot = pl.program_id(0)

    @pl.when(slot == 0)
    def _():
        tot12_ref[...] = jnp.sum(r_ref[...], axis=0)

    table = tot_ref[...]
    count = count_of(table, slot)
    mask = over_lanes(slot_mask0(meta, slot), M0)
    mean1, scale1 = mean_scale(table[:, :M0], slot, count)
    normed1 = (z1_ref[0] - mean1) * scale1
    d1 = norm_back(g1_ref[0], normed1, scale1, n_ref[0:1, :M0], tot12_ref[...], slot, count, mask)
    d1_ref[0] = d1
    grad = dot_nt(d1, w_ref[...]) + placed(g0_ref[0])
    gx_ref[0] = grad.astype(BF16).reshape(HB, WB, C0)


def unpack_body(cols, rows, i_ref, o_ref):
    tiles = cols // 128
    for tile in range(tiles):
        part = i_ref[pl.ds(tile, rows, stride=tiles), :]
        o_ref[:, tile * 128 : (tile + 1) * 128] = part.astype(BF16)


def unpack(packed, offset, rows, cols, steps):
    flat = packed[:, offset : offset + rows * cols].astype(F32).reshape(-1, 128)
    part = rows // steps
    return pl.pallas_call(
        functools.partial(unpack_body, cols, part),
        out_shape=shape_of((rows, cols), BF16),
        grid=(steps,),
        in_specs=[pl.BlockSpec((part * cols // 128, 128), lambda i: (i, 0))],
        out_specs=pl.BlockSpec((part, cols), lambda i: (i, 0)),
    )(flat)


def pack_body(cols, rows, i_ref, o_ref):
    tiles = cols // 128
    for tile in range(tiles):
        o_ref[pl.ds(tile, rows, stride=tiles), :] = i_ref[:, tile * 128 : (tile + 1) * 128].astype(F32)


def pack(matrix, steps):
    rows, cols = matrix.shape
    part = rows // steps
    return pl.pallas_call(
        functools.partial(pack_body, cols, part),
        out_shape=shape_of((rows * cols // 128, 128), F32),
        grid=(steps,),
        in_specs=[pl.BlockSpec((part, cols), lambda i: (i, 0))],
        out_specs=pl.BlockSpec((part * cols // 128, 128), lambda i: (i, 0)),
    )(matrix).reshape(-1)


def swap_cores(value):
    return lax.ppermute(value, "pipe", [(0, 1), (1, 0)])


def spread(value):
    count = lax.axis_size("dp")
    copies = jnp.broadcast_to(value[None], (count,) + value.shape)
    return lax.all_to_all(copies, "dp", 0, 0)


def summed(value):
    count = lax.axis_size("dp")
    if count != 16:
        return lax.psum(value, "dp")
    for step in (1, 4):
        parts = [
            lax.ppermute(value, "dp", [(i, i ^ (k * step)) for i in range(count)]) for k in (1, 2, 3)
        ]
        value = (value + parts[0]) + (parts[1] + parts[2])
    return value


def halved(value, axis_bits):
    count = lax.axis_size("dp")
    me = lax.axis_index("dp")
    for bit in axis_bits:
        half = value.shape[0] // 2
        mine = (me & bit) != 0
        kept = jnp.where(mine, value[half:], value[:half])
        sent = jnp.where(mine, value[:half], value[half:])
        got = lax.ppermute(sent, "dp", [(i, i ^ bit) for i in range(count)])
        value = (kept.astype(F32) + got.astype(F32)).astype(BF16)
    return value


def doubled(value, axis_bits):
    count = lax.axis_size("dp")
    me = lax.axis_index("dp")
    for bit in reversed(axis_bits):
        got = lax.ppermute(value, "dp", [(i, i ^ bit) for i in range(count)])
        mine = (me & bit) != 0
        value = jnp.concatenate([jnp.where(mine, got, value), jnp.where(mine, value, got)], axis=0)
    return value


def panels(matrix):
    return [matrix[:, k : k + 256] for k in range(0, matrix.shape[1], 256)]


def grad_of(left, right):
    return lax.dot_general(
        left, right, (((0,), (0,)), ((), ())), preferred_element_type=F32
    ).astype(BF16)


def conv_grad(padded_rows, delta, breadth, pixels):
    pieces = [
        grad_of(padded_rows[:, a * breadth : a * breadth + pixels].reshape(-1, padded_rows.shape[2]), delta)
        for a in range(3)
    ]
    return jnp.concatenate(pieces, axis=0)


def on_device(images, extents, views, params, norms, cotangent):
    core = lax.axis_index("pipe")
    first_core = core == 0
    count = lax.axis_size("dp")
    bits = [1 << k for k in range(count.bit_length() - 1)]

    own_views = lax.dynamic_slice(views, (core * SLOTS,), (SLOTS,))
    own_ext = lax.dynamic_slice(extents, (core * SLOTS, 0), (SLOTS, 2))
    order = []
    for mb in range(SLOTS // IMG_MB):
        flipped = own_views[2 * mb] != 0
        order += [jnp.where(flipped, 2 * mb + 1, 2 * mb), jnp.where(flipped, 2 * mb, 2 * mb + 1)]
    order = jnp.stack(order).astype(jnp.int32)
    hot = (order[:, None] == jnp.arange(SLOTS, dtype=jnp.int32)[None, :]).astype(jnp.int32)
    sizes = jnp.sum(hot[:, :, None] * own_ext[None], axis=1)
    meta = jnp.concatenate([order + core * SLOTS, sizes[:, 0], sizes[:, 1], order]).astype(jnp.int32)

    norms_there = swap_cores(norms[0])
    norms0 = jnp.where(first_core, norms[0], norms_there)
    norms1 = jnp.where(first_core, norms_there, norms[0])

    def from_core(owner, matrix):
        got = lax.ppermute(matrix, "pipe", [(owner, 1 - owner)])
        return jnp.where(core == owner, matrix, got)

    w1 = from_core(0, unpack(params, 0, C0, M0, 2))
    w2 = from_core(0, unpack(params, 262144, 9 * M0, M0, 3))
    w3 = from_core(0, unpack(params, 851968, M0, C0, 2))
    v1 = from_core(1, unpack(params, 0, C0, M1, 2))
    v2 = from_core(1, unpack(params, 524288, 9 * M1, M1, 6))
    v3 = from_core(1, unpack(params, 2883584, M1, C1, 4))
    vs = from_core(1, unpack(params, 3932160, C0, C1, 8))

    image = per_image(HB, WB, C0)
    z1, st = call(
        front_one,
        [shape_of((SLOTS, PIX0, M0), F32), shape_of((8, M0 + 128), F32)],
        (SLOTS,),
        [image, full(C0, M0)],
        [per_slot(PIX0, M0), full(8, M0 + 128)],
    )(meta, images, w1)
    tot1, act, z2, st = call(
        front_two,
        [
            shape_of((8, M0 + 128), F32),
            shape_of((SLOTS, PIX0 + 2 * WB, 3 * M0), BF16),
            shape_of((SLOTS, PIX0, M0), F32),
            shape_of((8, M0), F32),
        ],
        (SLOTS,),
        [full(count, 8, M0 + 128), per_slot(PIX0, M0), full(2, CN), full(9 * M0, M0)],
        [full(8, M0 + 128), per_slot(PIX0 + 2 * WB, 3 * M0), per_slot(PIX0, M0), full(8, M0)],
    )(meta, spread(st), z1, norms0, w2)
    tot2, a2, st = call(
        front_three,
        [shape_of((8, M0), F32), shape_of((SLOTS, PIX0, M0), BF16), shape_of((8, C0), F32)],
        (SLOTS,),
        [
            full(count, 8, M0),
            full(8, M0 + 128),
            per_slot(PIX0, M0),
            full(2, CN),
            full(M0, C0),
        ],
        [full(8, M0), per_slot(PIX0, M0), full(8, C0)],
    )(meta, spread(st), tot1, z2, norms0, w3)
    tot3 = summed(st)

    clamp = lambda s: jnp.minimum(s, SLOTS - 1)
    tile = lambda s: jnp.maximum(s - SLOTS, 0)
    rows1 = SLOTS * PIX1
    src, p_even, z3_even, y1, ys, st, sts = call(
        join,
        [
            shape_of((rows1, C0), BF16),
            shape_of((rows1, C0), F32),
            shape_of((rows1, C0), F32),
            shape_of((rows1, M1), F32),
            shape_of((rows1, C1), F32),
            shape_of((8, M1), F32),
            shape_of((8, C1), F32),
        ],
        (SLOTS + 4,),
        [
            full(8, C0),
            full(8, M0 + 128),
            pl.BlockSpec((1, PIX0, M0), lambda s, meta: (clamp(s), 0, 0)),
            pl.BlockSpec((1, HB, WB, C0), lambda s, meta: (meta[clamp(s)], 0, 0, 0)),
            full(2, CN),
            full(M0, C0),
            full(C0, M1),
            pl.BlockSpec((C0, C1 // 4), lambda s, meta: (0, tile(s))),
        ],
        [
            full(rows1, C0),
            full(rows1, C0),
            full(rows1, C0),
            full(rows1, M1),
            pl.BlockSpec((rows1, C1 // 4), lambda s, meta: (0, tile(s))),
            full(8, M1),
            pl.BlockSpec((8, C1 // 4), lambda s, meta: (0, tile(s))),
        ],
    )(meta, tot3, tot1, a2, images, norms0, w3, v1, vs)
    tots = summed(sts)

    one = (1,)
    tot4, act1, y2, st = call(
        mid_one,
        [
            shape_of((8, M1), F32),
            shape_of((rows1, 3 * M1), BF16),
            shape_of((rows1, M1), F32),
            shape_of((8, M1), F32),
        ],
        one,
        [full(count, 8, M1), full(8, M0 + 128), full(rows1, M1), full(2, CN), full(9 * M1, M1)],
        [full(8, M1), full(rows1, 3 * M1), full(rows1, M1), full(8, M1)],
    )(meta, spread(st), tot1, y1, norms1, v2)
    tot5, b2, y3, st = call(
        mid_two,
        [
            shape_of((8, M1), F32),
            shape_of((rows1, M1), BF16),
            shape_of((rows1, C1), F32),
            shape_of((8, C1), F32),
        ],
        one,
        [full(count, 8, M1), full(8, M0 + 128), full(rows1, M1), full(2, CN), full(M1, C1)],
        [full(8, M1), full(rows1, M1), full(rows1, C1), full(8, C1)],
    )(meta, spread(st), tot1, y2, norms1, v3)
    tot6 = summed(st)

    by_image = pl.BlockSpec(
        (1, HB // 2, WB // 2, C1), lambda s, meta: (meta[3 * SLOTS + s], 0, 0, 0)
    )
    y_out, grad_y, st, stg = call(
        turn,
        [
            shape_of((SLOTS, HB // 2, WB // 2, C1), BF16),
            shape_of((SLOTS, PIX1, C1), F32),
            shape_of((8, C1), F32),
            shape_of((8, C1), F32),
        ],
        (SLOTS,),
        [
            full(8, C1),
            full(8, C1),
            full(8, M0 + 128),
            per_slot(PIX1, C1),
            per_slot(PIX1, C1),
            full(2, CN),
            per_image(HB // 2, WB // 2, C1),
        ],
        [by_image, per_slot(PIX1, C1), full(8, C1), full(8, C1)],
    )(
        meta, tot6, tots, tot1, y3.reshape(SLOTS, PIX1, C1), ys.reshape(SLOTS, PIX1, C1),
        norms1, cotangent,
    )
    tot7 = summed(st)
    totg = summed(stg)
    grad_y = grad_y.reshape(rows1, C1)

    e3, g2, st = call(
        back_one,
        [shape_of((rows1, C1), BF16), shape_of((rows1, M1), F32), shape_of((8, M1), F32)],
        one,
        [
            full(8, C1), full(8, C1), full(8, M1), full(8, M0 + 128), full(rows1, C1),
            full(rows1, C1), full(rows1, M1), full(2, CN), full(M1, C1),
        ],
        [full(rows1, C1), full(rows1, M1), full(8, M1)],
    )(meta, tot7, tot6, tot5, tot1, y3, grad_y, y2, norms1, v3)
    tot8, e2, g1, st = call(
        back_two,
        [
            shape_of((8, M1), F32),
            shape_of((rows1, M1), BF16),
            shape_of((rows1, M1), F32),
            shape_of((8, M1), F32),
        ],
        one,
        [
            full(count, 8, M1), full(8, M1), full(8, M1), full(8, M0 + 128), full(rows1, M1),
            full(rows1, M1), full(rows1, M1), full(2, CN), full(9 * M1, M1),
        ],
        [full(8, M1), full(rows1, M1), full(rows1, M1), full(8, M1)],
    )(meta, spread(st), tot5, tot4, tot1, y2, g2, y1, norms1, v2)
    tot9, e1, es, g0, st = call(
        back_three,
        [
            shape_of((8, M1), F32),
            shape_of((rows1, M1), BF16),
            shape_of((rows1, C1), BF16),
            shape_of((rows1, C0), F32),
            shape_of((8, C0), F32),
        ],
        one,
        [
            full(count, 8, M1), full(8, M1), full(8, M0 + 128), full(rows1, M1), full(rows1, M1),
            full(8, C1), full(8, C1), full(rows1, C1), full(rows1, C1), full(8, C0),
            full(rows1, C0), full(rows1, C0), full(2, CN), full(2, CN), full(C0, M1), full(C0, C1),
        ],
        [full(8, M1), full(rows1, M1), full(rows1, C1), full(rows1, C0), full(8, C0)],
    )(
        meta, spread(st), tot4, tot1, y1, g1, totg, tots, ys, grad_y, tot3, p_even, z3_even,
        norms0, norms1, v1, vs,
    )
    tot10 = summed(st)
    g0 = g0.reshape(SLOTS, PIX1, C0)

    d3, g2, st = call(
        last_one,
        [
            shape_of((SLOTS, PIX0, C0), BF16),
            shape_of((SLOTS, PIX0, M0), F32),
            shape_of((8, M0), F32),
        ],
        (SLOTS,),
        [
            full(8, C0), full(8, C0), full(8, M0), full(8, M0 + 128), per_slot(PIX0, M0),
            per_slot(PIX1, C0), per_slot(PIX0, M0), full(2, CN), full(M0, C0),
        ],
        [per_slot(PIX0, C0), per_slot(PIX0, M0), full(8, M0)],
    )(meta, tot10, tot3, tot2, tot1, a2, g0, z2, norms0, w3)
    tot11, d2, g1, st = call(
        last_two,
        [
            shape_of((8, M0), F32),
            shape_of((SLOTS, PIX0, M0), BF16),
            shape_of((SLOTS, PIX0, M0), F32),
            shape_of((8, M0), F32),
        ],
        (SLOTS,),
        [
            full(count, 8, M0), full(8, M0), full(8, M0 + 128), per_slot(PIX0, M0),
            per_slot(PIX0, M0), per_slot(PIX0, M0), full(2, CN), full(9 * M0, M0),
        ],
        [full(8, M0), per_slot(PIX0, M0), per_slot(PIX0, M0), full(8, M0)],
    )(meta, spread(st), tot2, tot1, z2, g2, z1, norms0, w2)
    own_image = pl.BlockSpec((1, HB, WB, C0), lambda s, meta: (meta[3 * SLOTS + s], 0, 0, 0))
    tot12, d1, gx = call(
        last_three,
        [
            shape_of((8, M0), F32),
            shape_of((SLOTS, PIX0, M0), BF16),
            shape_of((SLOTS, HB, WB, C0), BF16),
        ],
        (SLOTS,),
        [
            full(count, 8, M0), full(8, M0 + 128), per_slot(PIX0, M0), per_slot(PIX0, M0),
            per_slot(PIX1, C0), full(2, CN), full(C0, M0),
        ],
        [full(8, M0), per_slot(PIX0, M0), own_image],
    )(meta, spread(st), tot1, z1, g1, g0, norms0, w1)

    own = lax.dynamic_slice_in_dim(images, core * SLOTS, SLOTS, 0)
    picked = jnp.take(own, order, axis=0).reshape(SLOTS * PIX0, C0)
    flat_d2 = d2.reshape(SLOTS * PIX0, M0)
    wide1 = jnp.pad(act1.reshape(SLOTS, PIX1, 3 * M1), ((0, 0), (8, 8), (0, 0)))
    grads0 = [
        grad_of(picked, d1.reshape(SLOTS * PIX0, M0)),
        conv_grad(act, flat_d2, WB, PIX0),
        grad_of(a2.reshape(SLOTS * PIX0, M0), d3.reshape(SLOTS * PIX0, C0)),
    ]
    grads1 = [
        grad_of(src, e1),
        conv_grad(wide1, e2, WB // 2, PIX1),
        grad_of(b2, e3),
        grad_of(src, es),
    ]
    pieces = []
    for matrix in grads1 + grads0:
        pieces += panels(matrix)
    joined = jnp.concatenate(pieces, axis=0)
    padding = -joined.shape[0] % (64 * count)
    joined = jnp.pad(joined, ((0, padding), (0, 0)))
    half = joined.shape[0] // 2
    kept = jnp.where(first_core, joined[:half], joined[half:])
    other = swap_cores(jnp.where(first_core, joined[half:], joined[:half]))
    shard = (kept.astype(F32) + other.astype(F32)).astype(BF16)
    shard = doubled(halved(shard, bits), bits)
    other = swap_cores(shard)
    whole = jnp.concatenate(
        [jnp.where(first_core, shard, other), jnp.where(first_core, other, shard)], axis=0
    )

    def packed_grads(start, shapes):
        flats = []
        for rows, cols in shapes:
            parts = []
            for _ in range(0, cols, 256):
                parts.append(whole[start : start + rows])
                start += rows
            flats.append(pack(jnp.concatenate(parts, axis=1), max(1, rows * cols // 262144)))
        flat = jnp.concatenate(flats)
        return jnp.pad(flat, (0, P_SIZE - flat.shape[0]))

    shapes1 = [(C0, M1), (9 * M1, M1), (M1, C1), (C0, C1)]
    shapes0 = [(C0, M0), (9 * M0, M0), (M0, C0)]
    rows_one = P_SIZE // 256
    weight_grads = lax.cond(
        first_core,
        lambda: packed_grads(rows_one, shapes0),
        lambda: packed_grads(0, shapes1),
    )

    def gain_shift(table):
        parts = table.reshape(SLOTS, 2, -1).sum(axis=0)
        return jnp.stack([parts[1], parts[0]])

    line0 = jnp.concatenate([gain_shift(tot12), gain_shift(tot11), gain_shift(tot10)], axis=1)
    line0 = jnp.pad(line0, ((0, 0), (0, CN - line0.shape[1])))
    line1 = jnp.concatenate(
        [gain_shift(tot9), gain_shift(tot8), gain_shift(tot7), gain_shift(totg)], axis=1
    )
    got = swap_cores(jnp.where(first_core, line1, line0))
    norm_grads = jnp.where(first_core, line0, line1) + got

    elems = HB * WB * C0
    rows_y = jnp.pad(y_out.reshape(SLOTS, -1), ((0, 0), (0, elems // 2)))
    rows_x = gx.reshape(SLOTS, -1)
    got = swap_cores(jnp.where(first_core, rows_y, rows_x))
    boundary = jnp.concatenate(
        [jnp.where(first_core, rows_x, got), jnp.where(first_core, got, rows_y)], axis=0
    )
    return boundary[None], weight_grads[None], norm_grads[None]


def solution(mesh):
    placed_as = (
        P("dp", None, None, None),
        P("dp", None),
        P("dp"),
        P("pipe", None),
        P("pipe", None, None),
        P("dp", None, None, None),
    )
    return jax.shard_map(
        on_device,
        mesh=mesh,
        in_specs=placed_as,
        out_specs=(P("pipe", "dp", None), P("pipe", None), P("pipe", None, None)),
        check_vma=False,
    )
```

time: 4240 us -> 933 us (0.22)
  the two profiles are of different devices: /device:TPU:0 before, /device:TPU:1 now
where the time goes in v1:
time: 933 us; the launch traced here: 920 us
  waiting for transfers between devices  358 us (38%)
  other arithmetic  194 us (21%)
  starting transfers between devices  136 us (15%)
  local copies, waits for them, and re-layouts  106 us (11%)
  Pallas kernels  102 us (11%)
  matrix products  21.5 us (2%)
    ppermute x4, waiting for transfers between devices, halved(): got = lax.ppermute(sent, 'dp', [(i, i ^ bit) for i in range(count)])  155 us
    ppermute x4, waiting for transfers between devices, doubled(): got = lax.ppermute(value, 'dp', [(i, i ^ bit) for i in range(count)])  142 us
    unnamed x213, local copies, waits for them, and re-layouts  66.9 us
    all_to_all x8, starting transfers between devices, spread(): return lax.all_to_all(copies, 'dp', 0, 0)  47.2 us
    reshape x6, other arithmetic, unpack(): flat = packed[:, offset:offset + rows * cols].astype(F32).reshape(-1, 128)  46.2 us
    ppermute x36, starting transfers between devices, summed(): lax.ppermute(value, 'dp', [(i, i ^ k * step) for i in range(count)])  38.1 us
    all_to_all x8, waiting for transfers between devices, spread(): return lax.all_to_all(copies, 'dp', 0, 0)  33.4 us
    pallas_call x7, Pallas kernels, unpack(): pl.pallas_call(functools.partial(unpack_body, cols, part), out_shape=shap...  31 us
  transfers between devices with their start and end apart: 64, of which 22 were waited for; matrix products, arithmetic and copies ran while one was open for 14% of the time, Pallas kernels for 6%

profile of v1, /device:TPU:1, one launch (start us, length us, event | category | flops | bytes accessed | tf_op | source)
XLA Modules:
  0.0 920.4 jit_solution(4738695611728059305)
XLA Ops:
  20.0 10.8 %slice_convert_fusion.1 = f32[1,2097152]{1,0:T(1,128)} fusion(bf16[1,6029312]{1,0:T(2,128)(2,1)} %param.11), kind=kLoop, calls=%fused_computation.28 | loop fusion | flops 2097152 | bytes 12582912 | tf_op jit(solution)/shard_map/reshape | solution.py:526
  30.8 8.7 shard_map.92
  39.5 6.0 collective-permute-start.11
  45.5 11.9 %slice_convert_fusion = f32[1,2359296]{1,0:T(1,128)} fusion(bf16[1,6029312]{1,0:T(2,128)(2,1)} %param.11), kind=kLoop, calls=%fused_computation.27 | loop fusion | flops 2359296 | bytes 14155776 | tf_op jit(solution)/shard_map/reshape | solution.py:526
  57.5 7.4 shard_map.94
  75.1 8.6 slice_convert_fusion.2
  101.8 7.4 all-to-all-start
  110.6 6.6 all-to-all-done.r_ref
  156.9 7.6 collective-permute-start.13
  169.3 7.4 shard_map.93
  282.1 15.7 %all-to-all-start.5 = ((f32[16,8,512]{2,1,0:T(8,128)}), f32[16,8,512]{2,1,0:T(8,128)}, u32[]{:S(2)}, u32[]{:S(2)}) async-start(f32[16,8,512]{2,1,0:T(8,128)} %broadcast_in_dim.38), calls=%async_computation.5 | async-start | bytes 524288 | tf_op jit(solution)/shard_map/all_to_all | solution.py:562
  396.9 7.4 broadcast_select_fusion.2
  404.3 14.5 %collective-permute-start.45 = (bf16[14336,256]{1,0:T(8,128)(2,1)}, bf16[14336,256]{1,0:T(8,128)(2,1)}, u32[]{:S(2)}, u32[]{:S(2)}) collective-permute-start(bf16[14336,256]{1,0:T(8,128)(2,1)} %broadcast_select_fusion.2), channel_id=1, source_target_pairs={{0,16},{16,0},{1,17},{17,1},{2,18},{18,2},{3,19},{19,3},{4,20},{20... | collective-permute-start | bytes 22020104 | tf_op jit(solution)/shard_map/ppermute | solution.py:556
  418.8 11.6 %collective-permute-done.45 = bf16[14336,256]{1,0:T(8,128)(2,1)} collective-permute-done((bf16[14336,256]{1,0:T(8,128)(2,1)}, bf16[14336,256]{1,0:T(8,128)(2,1)}, u32[]{:S(2)}, u32[]{:S(2)}) %collective-permute-start.45) | collective-permute-done | bytes 7340064 | tf_op jit(solution)/shard_map/ppermute | solution.py:556
  430.4 6.7 add_convert_fusion
  442.2 78.4 %collective-permute-done.46 = bf16[7168,256]{1,0:T(8,128)(2,1)} collective-permute-done((bf16[7168,256]{1,0:T(8,128)(2,1)}, bf16[7168,256]{1,0:T(8,128)(2,1)}, u32[]{:S(2)}, u32[]{:S(2)}) %collective-permute-start.46) | collective-permute-done | bytes 3670048 | tf_op jit(solution)/shard_map/ppermute | solution.py:585
  528.4 38.3 %collective-permute-done.47 = bf16[3584,256]{1,0:T(8,128)(2,1)} collective-permute-done((bf16[3584,256]{1,0:T(8,128)(2,1)S(1)}, bf16[3584,256]{1,0:T(8,128)(2,1)}, u32[]{:S(2)}, u32[]{:S(2)}) %collective-permute-start.47) | collective-permute-done | bytes 1835040 | tf_op jit(solution)/shard_map/ppermute | solution.py:585
  571.5 17.9 %collective-permute-done.48 = bf16[1792,256]{1,0:T(8,128)(2,1)} collective-permute-done((bf16[1792,256]{1,0:T(8,128)(2,1)}, bf16[1792,256]{1,0:T(8,128)(2,1)}, u32[]{:S(2)}, u32[]{:S(2)}) %collective-permute-start.48) | collective-permute-done | bytes 917536 | tf_op jit(solution)/shard_map/ppermute | solution.py:585
  595.3 20.7 %collective-permute-done.49 = bf16[896,256]{1,0:T(8,128)(2,1)} collective-permute-done((bf16[896,256]{1,0:T(8,128)(2,1)}, bf16[896,256]{1,0:T(8,128)(2,1)}, u32[]{:S(2)}, u32[]{:S(2)}) %collective-permute-start.49) | collective-permute-done | bytes 458784 | tf_op jit(solution)/shard_map/ppermute | solution.py:585
  618.2 20.7 %collective-permute-done.50 = bf16[896,256]{1,0:T(8,128)(2,1)} collective-permute-done((bf16[896,256]{1,0:T(8,128)(2,1)S(1)}, bf16[896,256]{1,0:T(8,128)(2,1)}, u32[]{:S(2)}, u32[]{:S(2)}) %collective-permute-start.50) | collective-permute-done | bytes 458784 | tf_op jit(solution)/shard_map/ppermute | solution.py:594
  643.5 19.4 %collective-permute-done.51 = bf16[1792,256]{1,0:T(8,128)(2,1)} collective-permute-done((bf16[1792,256]{1,0:T(8,128)(2,1)}, bf16[1792,256]{1,0:T(8,128)(2,1)}, u32[]{:S(2)}, u32[]{:S(2)}) %collective-permute-start.51) | collective-permute-done | bytes 917536 | tf_op jit(solution)/shard_map/ppermute | solution.py:594
  665.0 6.5 pad_select_fusion.1
  673.9 30.9 %collective-permute-done.52 = bf16[3584,256]{1,0:T(8,128)(2,1)S(1)} collective-permute-done((bf16[3584,256]{1,0:T(8,128)(2,1)S(1)}, bf16[3584,256]{1,0:T(8,128)(2,1)S(1)}, u32[]{:S(2)}, u32[]{:S(2)}) %collective-permute-start.52) | collective-permute-done | bytes 1835040 | tf_op jit(solution)/shard_map/ppermute | solution.py:594
  706.0 6.7 broadcast_select_fusion.10
  712.7 71.5 %collective-permute-done.53 = bf16[7168,256]{1,0:T(8,128)(2,1)S(1)} collective-permute-done((bf16[7168,256]{1,0:T(8,128)(2,1)S(1)}, bf16[7168,256]{1,0:T(8,128)(2,1)S(1)}, u32[]{:S(2)}, u32[]{:S(2)}) %collective-permute-start.53) | collective-permute-done | bytes 3670048 | tf_op jit(solution)/shard_map/ppermute | solution.py:594
  785.7 20.5 %pad_maximum_fusion.4 = bf16[14336,256]{1,0:T(8,128)(2,1)S(1)} fusion(bf16[7168,256]{1,0:T(8,128)(2,1)S(1)} %get-tuple-element.138, bf16[7168,256]{1,0:T(8,128)(2,1)S(1)} %get-tuple-element.137), kind=kLoop, calls=%fused_computation.29 | loop fusion | flops 14680064 | bytes 14680064 | tf_op jit(solution)/shard_map/concatenate | solution.py:596
  812.8 7.9 collective-permute-done.54
  820.7 21.2 %broadcast_select_fusion.1 = bf16[14336,256]{1,0:T(8,128)(2,1)S(1)} fusion(bf16[14336,256]{1,0:T(8,128)(2,1)S(1)} %collective-permute-done.54, pred[]{:T(512)} %eq.14, bf16[7168,256]{1,0:T(8,128)(2,1)S(1)} %get-tuple-element.138, bf16[7168,256]{1,0:T(8,128)(2,1)S(1)} %get-tuple-element.137), kind=kLoop, calls=%fused_computation.31 | loop fusion | flops 18350080 | bytes 22020096 | tf_op jit(solution)/shard_map/jit(_where)/select_n | solution.py:901
  841.9 77.4 %conditional.1 = (f32[1,6029312]{1,0:T(1,128)}) conditional(s32[]{:T(128)} %convert_element_type.106, (pred[]{:T(512)}, bf16[14336,256]{1,0:T(8,128)(2,1)S(1)}, bf16[14336,256]{1,0:T(8,128)(2,1)S(1)}, bf16[14336,256]{1,0:T(8,128)(2,1)S(1)}) %tuple.16, bf16[14336,256]{1,0:T(8,128)(2,1)S(1)} %broadcast_select_fusion.1), branch_computations={%region_1.2_spmd, %region_2.3_spmd} | conditional | flops 38273024 | bytes 173015136 | solution.py:918
  869.0 9.1 branch_0_fun.7
  883.4 8.5 branch_0_fun.5
  896.7 22.7 %pad_maximum_fusion = f32[6029312]{0:T(1024)} fusion(f32[2097152]{0:T(1024)} %bitcast.102, f32[1048576]{0:T(1024)} %bitcast.109, f32[2359296]{0:T(1024)} %bitcast.100, f32[524288]{0:T(1024)} %bitcast.115), kind=kLoop, calls=%fused_computation.1 | loop fusion | flops 18087936 | bytes 48234496 | tf_op jit(solution)/shard_map/cond/branch_0_fun/concatenate | solution.py:912
  (467 shorter events, 377.3 us)
Async XLA Ops:
  7.0 85.1 %collective-permute-start = (bf16[1024,256]{1,0:T(8,128)(2,1)}, bf16[1024,256]{1,0:T(8,128)(2,1)S(1)}, u32[]{:S(2)}, u32[]{:S(2)}) collective-permute-start(bf16[1024,256]{1,0:T(8,128)(2,1)} %shard_map.85), channel_id=1, source_target_pairs={{0,16},{1,17},{2,18},{3,19},{4,20},{5,21},{6,22},{7,23},{8,24},{9,... | collective-permute-start | bytes 1572872 | tf_op jit(solution)/shard_map/ppermute | solution.py:640
  8.3 82.5 %collective-permute-start.1 = (f32[2,5120]{1,0:T(2,128)S(1)}, f32[2,5120]{1,0:T(2,128)S(1)}, u32[]{:S(2)}, u32[]{:S(2)}) collective-permute-start(f32[2,5120]{1,0:T(2,128)S(1)} %bitcast.124), channel_id=1, source_target_pairs={{0,16},{16,0},{1,17},{17,1},{2,18},{18,2},{3,19},{19,3},{4,20},{20... | collective-permute-start | bytes 122888 | tf_op jit(solution)/shard_map/ppermute | solution.py:556
  18.7 90.5 %collective-permute-start.2 = (bf16[2304,256]{1,0:T(8,128)(2,1)}, bf16[2304,256]{1,0:T(8,128)(2,1)}, u32[]{:S(2)}, u32[]{:S(2)}) collective-permute-start(bf16[2304,256]{1,0:T(8,128)(2,1)} %shard_map.87), channel_id=1, source_target_pairs={{0,16},{1,17},{2,18},{3,19},{4,20},{5,21},{6,22},{7,23},{8,24},{9,... | collective-permute-start | bytes 3538952 | tf_op jit(solution)/shard_map/ppermute | solution.py:640
  39.5 125.0 %collective-permute-start.11 = (bf16[1024,2048]{1,0:T(8,128)(2,1)}, bf16[1024,2048]{1,0:T(8,128)(2,1)}, u32[]{:S(2)}, u32[]{:S(2)}) collective-permute-start(bf16[1024,2048]{1,0:T(8,128)(2,1)} %shard_map.92), channel_id=1, source_target_pairs={{16,0},{17,1},{18,2},{19,3},{20,4},{21,5},{22,6},{23,7},{24,8},{25... | collective-permute-start | bytes 12582920 | tf_op jit(solution)/shard_map/ppermute | solution.py:640
  64.9 122.3 %collective-permute-start.12 = (bf16[4608,512]{1,0:T(8,128)(2,1)}, bf16[4608,512]{1,0:T(8,128)(2,1)}, u32[]{:S(2)}, u32[]{:S(2)}) collective-permute-start(bf16[4608,512]{1,0:T(8,128)(2,1)} %shard_map.94), channel_id=1, source_target_pairs={{16,0},{17,1},{18,2},{19,3},{20,4},{21,5},{22,6},{23,7},{24,8},{25... | collective-permute-start | bytes 14155784 | tf_op jit(solution)/shard_map/ppermute | solution.py:640
  90.7 36.9 %collective-permute-start.3 = (bf16[256,1024]{1,0:T(8,128)(2,1)}, bf16[256,1024]{1,0:T(8,128)(2,1)}, u32[]{:S(2)}, u32[]{:S(2)}) collective-permute-start(bf16[256,1024]{1,0:T(8,128)(2,1)} %shard_map.89), channel_id=1, source_target_pairs={{0,16},{1,17},{2,18},{3,19},{4,20},{5,21},{6,22},{7,23},{8,24},{9,... | collective-permute-start | bytes 1572872 | tf_op jit(solution)/shard_map/ppermute | solution.py:640
  92.1 63.0 %collective-permute-start.10 = (bf16[1024,512]{1,0:T(8,128)(2,1)}, bf16[1024,512]{1,0:T(8,128)(2,1)}, u32[]{:S(2)}, u32[]{:S(2)}) collective-permute-start(bf16[1024,512]{1,0:T(8,128)(2,1)} %shard_map.91), channel_id=1, source_target_pairs={{16,0},{17,1},{18,2},{19,3},{20,4},{21,5},{22,6},{23,7},{24,8},{25... | collective-permute-start | bytes 3145736 | tf_op jit(solution)/shard_map/ppermute | solution.py:640
  101.8 15.5 %all-to-all-start = ((f32[16,8,384]{2,1,0:T(8,128)}), f32[16,8,384]{2,1,0:T(8,128)S(1)}, u32[]{:S(2)}, u32[]{:S(2)}) async-start(f32[16,8,384]{2,1,0:T(8,128)} %broadcast_in_dim.33), calls=%async_computation | async-start | bytes 393216 | tf_op jit(solution)/shard_map/all_to_all | solution.py:562
  156.9 50.7 %collective-permute-start.13 = (bf16[512,2048]{1,0:T(8,128)(2,1)}, bf16[512,2048]{1,0:T(8,128)(2,1)}, u32[]{:S(2)}, u32[]{:S(2)}) collective-permute-start(bf16[512,2048]{1,0:T(8,128)(2,1)} %shard_map.96), channel_id=1, source_target_pairs={{16,0},{17,1},{18,2},{19,3},{20,4},{21,5},{22,6},{23,7},{24,8},{25... | collective-permute-start | bytes 6291464 | tf_op jit(solution)/shard_map/ppermute | solution.py:640
  180.0 39.9 %collective-permute-start.20 = (f32[8,2048]{1,0:T(8,128)S(1)}, f32[8,2048]{1,0:T(8,128)}, u32[]{:S(2)}, u32[]{:S(2)}) collective-permute-start(f32[8,2048]{1,0:T(8,128)S(1)} %get-tuple-element.84), channel_id=1, source_target_pairs={{0,1},{1,0},{2,3},{3,2},{4,5},{5,4},{6,7},{7,6},{8,9},{9,8},{10,11... | collective-permute-start | bytes 196616 | tf_op jit(solution)/shard_map/ppermute | solution.py:571
  180.8 40.8 %collective-permute-start.21 = (f32[8,2048]{1,0:T(8,128)S(1)}, f32[8,2048]{1,0:T(8,128)}, u32[]{:S(2)}, u32[]{:S(2)}) collective-permute-start(f32[8,2048]{1,0:T(8,128)S(1)} %get-tuple-element.84), channel_id=1, source_target_pairs={{0,2},{1,3},{2,0},{3,1},{4,6},{5,7},{6,4},{7,5},{8,10},{9,11},{10,... | collective-permute-start | bytes 196616 | tf_op jit(solution)/shard_map/ppermute | solution.py:571
  180.8 40.8 %collective-permute-start.22 = (f32[8,2048]{1,0:T(8,128)S(1)}, f32[8,2048]{1,0:T(8,128)}, u32[]{:S(2)}, u32[]{:S(2)}) collective-permute-start(f32[8,2048]{1,0:T(8,128)S(1)} %get-tuple-element.84), channel_id=1, source_target_pairs={{0,3},{1,2},{2,1},{3,0},{4,7},{5,6},{6,5},{7,4},{8,11},{9,10},{10,... | collective-permute-start | bytes 196616 | tf_op jit(solution)/shard_map/ppermute | solution.py:571
  183.4 12.8 %all-to-all-start.2 = ((f32[16,8,512]{2,1,0:T(8,128)}), f32[16,8,512]{2,1,0:T(8,128)S(1)}, u32[]{:S(2)}, u32[]{:S(2)}) async-start(f32[16,8,512]{2,1,0:T(8,128)} %broadcast_in_dim.35), calls=%async_computation.2 | async-start | bytes 524288 | tf_op jit(solution)/shard_map/all_to_all | solution.py:562
  250.9 16.3 %collective-permute-start.35 = (f32[8,2048]{1,0:T(8,128)}, f32[8,2048]{1,0:T(8,128)}, u32[]{:S(2)}, u32[]{:S(2)}) collective-permute-start(f32[8,2048]{1,0:T(8,128)} %add_add_fusion.1), channel_id=1, source_target_pairs={{0,4},{1,5},{2,6},{3,7},{4,0},{5,1},{6,2},{7,3},{8,12},{9,13},{10,... | collective-permute-start | bytes 196616 | tf_op jit(solution)/shard_map/ppermute | solution.py:571
  252.1 15.2 %collective-permute-start.36 = (f32[8,2048]{1,0:T(8,128)}, f32[8,2048]{1,0:T(8,128)}, u32[]{:S(2)}, u32[]{:S(2)}) collective-permute-start(f32[8,2048]{1,0:T(8,128)} %add_add_fusion.1), channel_id=1, source_target_pairs={{0,8},{1,9},{2,10},{3,11},{4,12},{5,13},{6,14},{7,15},{8,0},{9,1},... | collective-permute-start | bytes 196616 | tf_op jit(solution)/shard_map/ppermute | solution.py:571
  253.3 13.9 %collective-permute-start.37 = (f32[8,2048]{1,0:T(8,128)}, f32[8,2048]{1,0:T(8,128)}, u32[]{:S(2)}, u32[]{:S(2)}) collective-permute-start(f32[8,2048]{1,0:T(8,128)} %add_add_fusion.1), channel_id=1, source_target_pairs={{0,12},{1,13},{2,14},{3,15},{4,8},{5,9},{6,10},{7,11},{8,4},{9,5},... | collective-permute-start | bytes 196616 | tf_op jit(solution)/shard_map/ppermute | solution.py:571
  282.1 22.8 %all-to-all-start.5 = ((f32[16,8,512]{2,1,0:T(8,128)}), f32[16,8,512]{2,1,0:T(8,128)}, u32[]{:S(2)}, u32[]{:S(2)}) async-start(f32[16,8,512]{2,1,0:T(8,128)} %broadcast_in_dim.38), calls=%async_computation.5 | async-start | bytes 524288 | tf_op jit(solution)/shard_map/all_to_all | solution.py:562
  317.0 22.5 %collective-permute-start.38 = (f32[8,1024]{1,0:T(8,128)S(1)}, f32[8,1024]{1,0:T(8,128)S(1)}, u32[]{:S(2)}, u32[]{:S(2)}) collective-permute-start(f32[8,1024]{1,0:T(8,128)S(1)} %get-tuple-element.98), channel_id=1, source_target_pairs={{0,1},{1,0},{2,3},{3,2},{4,5},{5,4},{6,7},{7,6},{8,9},{9,8},{10,11... | collective-permute-start | bytes 98312 | tf_op jit(solution)/shard_map/ppermute | solution.py:571
  318.2 21.2 %collective-permute-start.39 = (f32[8,1024]{1,0:T(8,128)S(1)}, f32[8,1024]{1,0:T(8,128)S(1)}, u32[]{:S(2)}, u32[]{:S(2)}) collective-permute-start(f32[8,1024]{1,0:T(8,128)S(1)} %get-tuple-element.98), channel_id=1, source_target_pairs={{0,2},{1,3},{2,0},{3,1},{4,6},{5,7},{6,4},{7,5},{8,10},{9,11},{10,... | collective-permute-start | bytes 98312 | tf_op jit(solution)/shard_map/ppermute | solution.py:571
  318.2 21.2 %collective-permute-start.40 = (f32[8,1024]{1,0:T(8,128)S(1)}, f32[8,1024]{1,0:T(8,128)S(1)}, u32[]{:S(2)}, u32[]{:S(2)}) collective-permute-start(f32[8,1024]{1,0:T(8,128)S(1)} %get-tuple-element.98), channel_id=1, source_target_pairs={{0,3},{1,2},{2,1},{3,0},{4,7},{5,6},{6,5},{7,4},{8,11},{9,10},{10,... | collective-permute-start | bytes 98312 | tf_op jit(solution)/shard_map/ppermute | solution.py:571
  404.3 26.1 %collective-permute-start.45 = (bf16[14336,256]{1,0:T(8,128)(2,1)}, bf16[14336,256]{1,0:T(8,128)(2,1)}, u32[]{:S(2)}, u32[]{:S(2)}) collective-permute-start(bf16[14336,256]{1,0:T(8,128)(2,1)} %broadcast_select_fusion.2), channel_id=1, source_target_pairs={{0,16},{16,0},{1,17},{17,1},{2,18},{18,2},{3,19},{19,3},{4,20},{20... | collective-permute-start | bytes 22020104 | tf_op jit(solution)/shard_map/ppermute | solution.py:556
  441.3 79.2 %collective-permute-start.46 = (bf16[7168,256]{1,0:T(8,128)(2,1)}, bf16[7168,256]{1,0:T(8,128)(2,1)}, u32[]{:S(2)}, u32[]{:S(2)}) collective-permute-start(bf16[7168,256]{1,0:T(8,128)(2,1)} %broadcast_select_fusion.7), channel_id=1, source_target_pairs={{0,1},{1,0},{2,3},{3,2},{4,5},{5,4},{6,7},{7,6},{8,9},{9,8},{10,11... | collective-permute-start | bytes 11010056 | tf_op jit(solution)/shard_map/ppermute | solution.py:585
  527.9 38.8 %collective-permute-start.47 = (bf16[3584,256]{1,0:T(8,128)(2,1)S(1)}, bf16[3584,256]{1,0:T(8,128)(2,1)}, u32[]{:S(2)}, u32[]{:S(2)}) collective-permute-start(bf16[3584,256]{1,0:T(8,128)(2,1)S(1)} %broadcast_select_fusion.13), channel_id=1, source_target_pairs={{0,2},{1,3},{2,0},{3,1},{4,6},{5,7},{6,4},{7,5},{8,10},{9,11},{10,... | collective-permute-start | bytes 5505032 | tf_op jit(solution)/shard_map/ppermute | solution.py:585
  571.0 18.4 %collective-permute-start.48 = (bf16[1792,256]{1,0:T(8,128)(2,1)}, bf16[1792,256]{1,0:T(8,128)(2,1)}, u32[]{:S(2)}, u32[]{:S(2)}) collective-permute-start(bf16[1792,256]{1,0:T(8,128)(2,1)} %broadcast_select_fusion.18), channel_id=1, source_target_pairs={{0,4},{1,5},{2,6},{3,7},{4,0},{5,1},{6,2},{7,3},{8,12},{9,13},{10,... | collective-permute-start | bytes 2752520 | tf_op jit(solution)/shard_map/ppermute | solution.py:585
  592.7 23.3 %collective-permute-start.49 = (bf16[896,256]{1,0:T(8,128)(2,1)}, bf16[896,256]{1,0:T(8,128)(2,1)}, u32[]{:S(2)}, u32[]{:S(2)}) collective-permute-start(bf16[896,256]{1,0:T(8,128)(2,1)} %broadcast_select_fusion.23), channel_id=1, source_target_pairs={{0,8},{1,9},{2,10},{3,11},{4,12},{5,13},{6,14},{7,15},{8,0},{9,1},... | collective-permute-start | bytes 1376264 | tf_op jit(solution)/shard_map/ppermute | solution.py:585
  617.5 21.4 %collective-permute-start.50 = (bf16[896,256]{1,0:T(8,128)(2,1)S(1)}, bf16[896,256]{1,0:T(8,128)(2,1)}, u32[]{:S(2)}, u32[]{:S(2)}) collective-permute-start(bf16[896,256]{1,0:T(8,128)(2,1)S(1)} %add_convert_fusion.4), channel_id=1, source_target_pairs={{0,8},{1,9},{2,10},{3,11},{4,12},{5,13},{6,14},{7,15},{8,0},{9,1},... | collective-permute-start | bytes 1376264 | tf_op jit(solution)/shard_map/ppermute | solution.py:594
  641.1 21.7 %collective-permute-start.51 = (bf16[1792,256]{1,0:T(8,128)(2,1)}, bf16[1792,256]{1,0:T(8,128)(2,1)}, u32[]{:S(2)}, u32[]{:S(2)}) collective-permute-start(bf16[1792,256]{1,0:T(8,128)(2,1)} %pad_maximum_fusion.8), channel_id=1, source_target_pairs={{0,4},{1,5},{2,6},{3,7},{4,0},{5,1},{6,2},{7,3},{8,12},{9,13},{10,... | collective-permute-start | bytes 2752520 | tf_op jit(solution)/shard_map/ppermute | solution.py:594
  641.3 32.0 %collective-permute-start.55 = (f32[2,5120]{1,0:T(2,128)S(1)}, f32[2,5120]{1,0:T(2,128)S(1)}, u32[]{:S(2)}, u32[]{:S(2)}) collective-permute-start(f32[2,5120]{1,0:T(2,128)S(1)} %get-tuple-element.122), channel_id=1, source_target_pairs={{0,16},{16,0},{1,17},{17,1},{2,18},{18,2},{3,19},{19,3},{4,20},{20... | collective-permute-start | bytes 122888 | tf_op jit(solution)/shard_map/ppermute | solution.py:556
  664.5 40.2 %collective-permute-start.52 = (bf16[3584,256]{1,0:T(8,128)(2,1)S(1)}, bf16[3584,256]{1,0:T(8,128)(2,1)S(1)}, u32[]{:S(2)}, u32[]{:S(2)}) collective-permute-start(bf16[3584,256]{1,0:T(8,128)(2,1)S(1)} %pad_maximum_fusion.7), channel_id=1, source_target_pairs={{0,2},{1,3},{2,0},{3,1},{4,6},{5,7},{6,4},{7,5},{8,10},{9,11},{10,... | collective-permute-start | bytes 5505032 | tf_op jit(solution)/shard_map/ppermute | solution.py:594
  671.6 34.4 %collective-permute-start.44 = (bf16[4,262144]{1,0:T(4,128)(2,1)S(1)}, bf16[4,262144]{1,0:T(4,128)(2,1)S(1)}, u32[]{:S(2)}, u32[]{:S(2)}) collective-permute-start(bf16[4,262144]{1,0:T(4,128)(2,1)S(1)} %pad_select_fusion.1), channel_id=1, source_target_pairs={{0,16},{16,0},{1,17},{17,1},{2,18},{18,2},{3,19},{19,3},{4,20},{20... | collective-permute-start | bytes 6291464 | tf_op jit(solution)/shard_map/ppermute | solution.py:556
  705.7 78.6 %collective-permute-start.53 = (bf16[7168,256]{1,0:T(8,128)(2,1)S(1)}, bf16[7168,256]{1,0:T(8,128)(2,1)S(1)}, u32[]{:S(2)}, u32[]{:S(2)}) collective-permute-start(bf16[7168,256]{1,0:T(8,128)(2,1)S(1)} %pad_maximum_fusion.6), channel_id=1, source_target_pairs={{0,1},{1,0},{2,3},{3,2},{4,5},{5,4},{6,7},{7,6},{8,9},{9,8},{10,11... | collective-permute-start | bytes 11010056 | tf_op jit(solution)/shard_map/ppermute | solution.py:594
  806.2 14.5 %collective-permute-start.54 = (bf16[14336,256]{1,0:T(8,128)(2,1)S(1)}, bf16[14336,256]{1,0:T(8,128)(2,1)S(1)}, u32[]{:S(2)}, u32[]{:S(2)}) collective-permute-start(bf16[14336,256]{1,0:T(8,128)(2,1)S(1)} %pad_maximum_fusion.4), channel_id=1, source_target_pairs={{0,16},{16,0},{1,17},{17,1},{2,18},{18,2},{3,19},{19,3},{4,20},{20... | collective-permute-start | bytes 22020104 | tf_op jit(solution)/shard_map/ppermute | solution.py:556
  (129 other events, 1191.0 us)
